TPU v7x, 256 devices: a whole 4x4x8 slice. The times are simulated.
256 devices in a mesh: freq: 32 (over y_lo, z, core), rcv: 8 (over x, y_hi).
Axes of the slice: x: 4, y: 4 (y_hi: 2, y_lo: 2; y = y_hi * 2 + y_lo), z: 8, core: 2. Of those that a mesh axis runs over, the one named last changes fastest.
Arguments:
- reflection: bfloat16 [2, 1024, 256, 1024], P(None, 'freq', 'rcv'), may hold values from -0.25 to 0.25
- plus_init: float32 [2, 1024, 12288], P(None, 'freq', 'rcv'), may hold values from -6 to 6
- onset_receiver: int32 [256, 12], P('rcv'), may hold values from 128 to 768
- onset_source: int32 [1024, 12], P('rcv'), may hold values from 128 to 768
Outputs:
- focus_minus: float32 [2, 1024, 3072], P(None, 'freq', 'rcv')
- focus_plus: float32 [2, 1024, 12288], P(None, 'freq', 'rcv')
All inputs are finite; a program needn't handle non-finite values.
Results may differ from a plain program's by a relative error of at most 0.017.
Values may be sent and summed in bfloat16 or wider, within the bound.
A program may use at most 128 MiB of HBM per device.

v0:
```python
import math

import jax
import jax.numpy as jnp
from jax import lax
from jax.sharding import PartitionSpec as P

S = 1024
P_SIZE = 12
ITERS = 2


def build_tables(freq_count):
    time_count = 2 * freq_count
    freq_index = lax.broadcasted_iota(jnp.int32, (freq_count, freq_count), 0)
    time_index = lax.broadcasted_iota(jnp.int32, (freq_count, freq_count), 1)
    phases = freq_index * time_index % time_count
    angles = phases.astype(jnp.float32) * (2.0 * math.pi / time_count)
    return (jnp.cos(angles), jnp.sin(angles))


def window_traces(spectrum, onsets, cosines, sines):
    freq_count = spectrum.shape[1]
    time_count = 2 * freq_count
    first_row = lax.broadcasted_iota(jnp.int32, (freq_count, 1), 0) == 0
    weights = jnp.where(first_row, 1.0, 2.0).astype(jnp.float32) / time_count
    numbers = (((0,), (0,)), ((), ()))
    even_part = lax.dot_general(
        spectrum[0] * weights,
        cosines,
        numbers,
        precision=lax.Precision.HIGHEST,
        preferred_element_type=jnp.float32,
    )
    odd_part = -lax.dot_general(
        spectrum[1] * weights,
        sines,
        numbers,
        precision=lax.Precision.HIGHEST,
        preferred_element_type=jnp.float32,
    )
    time_row = lax.broadcasted_iota(jnp.int32, (1, freq_count), 1)
    inside = (time_row < onsets[:, None]) | (time_row > time_count - onsets[:, None])
    fold = jnp.where(time_row == 0, 1.0, 2.0).astype(jnp.float32)
    even_part = jnp.where(inside, even_part * fold, 0.0)
    odd_part = jnp.where(inside, odd_part * fold, 0.0)
    back = (((1,), (1,)), ((), ()))
    real_out = lax.dot_general(
        cosines,
        even_part,
        back,
        precision=lax.Precision.HIGHEST,
        preferred_element_type=jnp.float32,
    )
    imag_out = -lax.dot_general(
        sines, odd_part, back, precision=lax.Precision.HIGHEST, preferred_element_type=jnp.float32
    )
    return jnp.stack([real_out, imag_out])


def local(reflection, plus_init, onset_receiver, onset_source):
    freq_local = reflection.shape[1]
    recv_local = reflection.shape[2]
    freq_groups = lax.axis_size("freq")
    rcv_groups = lax.axis_size("rcv")
    freq_count = freq_local * freq_groups
    cosines, sines = build_tables(freq_count)
    minus_width = recv_local * P_SIZE
    plus_width = plus_init.shape[2]
    minus_piece = minus_width // freq_groups
    plus_piece = plus_width // freq_groups
    position = lax.axis_index("freq")
    onsets_minus = lax.dynamic_slice_in_dim(
        onset_receiver.reshape(minus_width), position * minus_piece, minus_piece
    )
    onsets_plus = lax.dynamic_slice_in_dim(
        onset_source.reshape(plus_width), position * plus_piece, plus_piece
    )
    plus = plus_init
    focus_minus = jnp.zeros((2, freq_local, minus_width), jnp.float32)
    for iteration in range(ITERS):
        plus_half = plus.astype(jnp.bfloat16)
        gathered = lax.all_gather(plus_half, "rcv", axis=2, tiled=True)
        sources = gathered.reshape(2, freq_local, S, P_SIZE)
        stacked = jnp.concatenate([sources[0], sources[1]], axis=2)
        first_term = jnp.einsum(
            "fms,fsq->fmq", reflection[0], stacked, preferred_element_type=jnp.float32
        )
        second_term = jnp.einsum(
            "fms,fsq->fmq", reflection[1], stacked, preferred_element_type=jnp.float32
        )
        raw_minus = jnp.stack(
            [
                first_term[..., :P_SIZE] - second_term[..., P_SIZE:],
                first_term[..., P_SIZE:] + second_term[..., :P_SIZE],
            ]
        ).reshape(2, freq_local, minus_width)
        in_time = lax.all_to_all(raw_minus, "freq", split_axis=2, concat_axis=1, tiled=True)
        windowed_minus = window_traces(in_time, onsets_minus, cosines, sines)
        focus_minus = lax.all_to_all(
            windowed_minus.astype(jnp.bfloat16), "freq", split_axis=1, concat_axis=2, tiled=True
        ).astype(windowed_minus.dtype)
        minus_half = focus_minus.astype(jnp.bfloat16).reshape(2, freq_local, recv_local, P_SIZE)
        stacked_minus = jnp.concatenate([minus_half[0], minus_half[1]], axis=2)
        first_back = jnp.einsum(
            "fms,fmq->fsq", reflection[0], stacked_minus, preferred_element_type=jnp.float32
        )
        second_back = jnp.einsum(
            "fms,fmq->fsq", reflection[1], stacked_minus, preferred_element_type=jnp.float32
        )
        partial_sum = jnp.stack(
            [
                first_back[..., :P_SIZE] + second_back[..., P_SIZE:],
                first_back[..., P_SIZE:] - second_back[..., :P_SIZE],
            ]
        )
        blocks = partial_sum.reshape(2, freq_local, rcv_groups, freq_groups, plus_piece)
        moved = lax.all_to_all(
            blocks.astype(jnp.bfloat16), "freq", split_axis=3, concat_axis=1, tiled=True
        ).astype(blocks.dtype)
        summed = lax.psum_scatter(
            moved.astype(jnp.bfloat16), "rcv", scatter_dimension=2, tiled=True
        ).astype(jnp.float32)
        spectrum = summed.reshape(2, freq_count, plus_piece)
        windowed_plus = window_traces(spectrum, onsets_plus, cosines, sines)
        plus = plus_init + lax.all_to_all(
            windowed_plus.astype(jnp.bfloat16), "freq", split_axis=1, concat_axis=2, tiled=True
        ).astype(windowed_plus.dtype)
    return (focus_minus, plus)


def solution(mesh):
    return jax.shard_map(
        local,
        mesh=mesh,
        in_specs=(
            P(None, "freq", "rcv", None),
            P(None, "freq", "rcv"),
            P("rcv", None),
            P("rcv", None),
        ),
        out_specs=(P(None, "freq", "rcv"), P(None, "freq", "rcv")),
        check_vma=False,
    )
```

profile of v0, /device:TPU:1, one launch (start us, length us, event | category | flops | bytes accessed | tf_op | source)
XLA Modules:
  0.0 1073.4 jit_solution(9939592525255281017)
XLA Ops:
  9.8 59.9 %all-gather.3.cloned.1.call-done = bf16[2,32,12288]{2,1,0:T(8,128)(2,1)} async-done(((bf16[2,32,1536]{2,1,0:T(8,128)(2,1)}), bf16[2,32,12288]{2,1,0:T(8,128)(2,1)}) %all-gather.3.cloned.1.call-update) | async-done | bytes 1572880 | tf_op jit(solution)/shard_map/all_gather | solution.py:83
  78.1 6.0 copy.176
  89.8 5.3 copy.177
  100.7 9.4 all-to-all-start
  110.3 8.3 all-to-all-done
  120.8 17.8 %fusion.191 = f32[12,1024]{1,0:T(8,128)S(1)} fusion(f32[1024,12]{0,1:T(8,128)S(1)} %squeeze.64, f32[1024]{0:T(1024)S(1)} %get-tuple-element.38, f32[1024]{0:T(1024)S(1)} %get-tuple-element.39, s32[12]{0:T(128)S(1)} %get-tuple-element.14, s32[12]{0:T(128)S(1)} %get-tuple-element.15), kind=kOutput, calls=%fused_computation.104 | convolution fusion | flops 165748736 | bytes 106592 | tf_op jit(solution)/shard_map/dot_general | solution.py:28
  138.6 20.9 %fusion.203 = bf16[1,1024,12]{1,2,0:T(8,128)(2,1)S(1)} fusion(f32[12,1024]{1,0:T(8,128)S(1)} %fusion.191), kind=kOutput, calls=%fused_computation.108 | convolution fusion | flops 165687296 | bytes 73728 | tf_op jit(solution)/shard_map/dot_general | solution.py:48
  159.7 17.7 %fusion.197 = f32[12,1024]{1,0:T(8,128)S(1)} fusion(f32[1024,12]{0,1:T(8,128)S(1)} %squeeze.65, f32[1024]{0:T(1024)S(1)} %get-tuple-element.38, f32[1024]{0:T(1024)S(1)} %get-tuple-element.39, s32[12]{0:T(128)S(1)} %get-tuple-element.14, s32[12]{0:T(128)S(1)} %get-tuple-element.15), kind=kOutput, calls=%fused_computation.106 | convolution fusion | flops 165761024 | bytes 106592 | tf_op jit(solution)/shard_map/dot_general | solution.py:35
  177.4 21.0 %fusion.206 = bf16[1,1024,12]{1,2,0:T(8,128)(2,1)S(1)} fusion(f32[12,1024]{1,0:T(8,128)S(1)} %fusion.197), kind=kOutput, calls=%fused_computation.109 | convolution fusion | flops 165699584 | bytes 73728 | tf_op jit(solution)/shard_map/dot_general | solution.py:55
  200.2 12.3 %all_to_all.114 = bf16[32,2,384]{2,1,0:T(2,128)(2,1)S(1)} all-to-all(bf16[32,2,384]{2,1,0:T(2,128)(2,1)S(1)} %reshape.117), channel_id=1, replica_groups=mesh['freq'=32,'rcv'=8] {'freq'}, dimensions={0} | all-to-all | bytes 98304 | tf_op jit(solution)/shard_map/all_to_all | solution.py:100
  230.5 7.4 copy.187
  237.8 6.7 stack.91
  244.5 5.9 pad_maximum_fusion
  250.4 8.1 copy.188
  258.5 9.3 reshape.119
  267.8 42.7 %all_to_all.115 = bf16[32,2,12288]{2,1,0:T(2,128)(2,1)S(1)} all-to-all(bf16[32,2,12288]{2,1,0:T(2,128)(2,1)S(1)} %reshape.119), channel_id=1, replica_groups=mesh['freq'=32,'rcv'=8] {'freq'}, dimensions={0} | all-to-all | bytes 3145728 | tf_op jit(solution)/shard_map/all_to_all | solution.py:118
  320.5 9.1 copy.189
  329.6 9.7 all_to_all.93
  340.3 95.3 %all-reduce.5.cloned.1.call-done = bf16[2,1024,8,1,48]{1,4,2,0,3:T(8,128)(2,1)} async-done(((bf16[2,1024,8,1,48]{1,4,2,0,3:T(8,128)(2,1)}), bf16[2,1024,8,1,48]{1,4,2,0,3:T(8,128)(2,1)}) %all-reduce.5.cloned.1.call-update) | async-done | bytes 1572880
  437.3 18.2 %fusion.137 = f32[48,1024]{1,0:T(8,128)S(1)} fusion(f32[2,1024,1,1,48]{1,4,3,2,0:T(8,128)S(1)} %get-tuple-element.22, f32[1024]{0:T(1024)S(1)} %get-tuple-element.38, f32[1024]{0:T(1024)S(1)} %get-tuple-element.39, s32[48]{0:T(128)S(1)} %get-tuple-element.12, s32[48]{0:T(128)S(1)} %get-tuple-element.13), kind=kOutput, calls=%fused_computation.86 | convolution fusion | flops 618954752 | bytes 402432 | tf_op jit(solution)/shard_map/dot_general | solution.py:28
  455.5 21.5 %fusion.143 = bf16[1,1024,48]{1,2,0:T(8,128)(2,1)S(1)} fusion(f32[48,1024]{1,0:T(8,128)S(1)} %fusion.137), kind=kOutput, calls=%fused_computation.88 | convolution fusion | flops 618708992 | bytes 294912 | tf_op jit(solution)/shard_map/dot_general | solution.py:48
  477.0 18.2 %fusion.131 = f32[48,1024]{1,0:T(8,128)S(1)} fusion(f32[2,1024,1,1,48]{1,4,2,0,3:T(8,128)S(1)} %get-tuple-element.23, f32[1024]{0:T(1024)S(1)} %get-tuple-element.38, f32[1024]{0:T(1024)S(1)} %get-tuple-element.39, s32[48]{0:T(128)S(1)} %get-tuple-element.12, s32[48]{0:T(128)S(1)} %get-tuple-element.13), kind=kOutput, calls=%fused_computation.84 | convolution fusion | flops 619003904 | bytes 402432 | tf_op jit(solution)/shard_map/dot_general | solution.py:35
  495.2 21.6 %fusion.146 = bf16[1,1024,48]{1,2,0:T(8,128)(2,1)S(1)} fusion(f32[48,1024]{1,0:T(8,128)S(1)} %fusion.131), kind=kOutput, calls=%fused_computation.89 | convolution fusion | flops 618758144 | bytes 294912 | tf_op jit(solution)/shard_map/dot_general | solution.py:55
  518.2 20.7 %all_to_all.116 = bf16[32,2,1536]{2,1,0:T(2,128)(2,1)S(1)} all-to-all(bf16[32,2,1536]{2,1,0:T(2,128)(2,1)S(1)} %reshape.121), channel_id=1, replica_groups=mesh['freq'=32,'rcv'=8] {'freq'}, dimensions={0} | all-to-all | bytes 393216 | tf_op jit(solution)/shard_map/all_to_all | solution.py:126
  543.1 50.5 %all-gather.5.cloned.1.call-done = bf16[2,32,12288]{2,1,0:T(8,128)(2,1)} async-done(((bf16[2,32,1536]{2,1,0:T(8,128)(2,1)}), bf16[2,32,12288]{2,1,0:T(8,128)(2,1)}) %all-gather.5.cloned.1.call-update) | async-done | bytes 1572880 | tf_op jit(solution)/shard_map/all_gather | solution.py:83
  601.9 6.0 copy.196
  613.7 5.3 copy.197
  623.9 18.1 %all_to_all.117 = f32[32,1,768]{2,1,0:T(1,128)S(1)} all-to-all(f32[32,1,768]{2,1,0:T(1,128)S(1)} %reshape.123), channel_id=1, replica_groups=mesh['freq'=32,'rcv'=8] {'freq'}, dimensions={0} | all-to-all | bytes 196608 | tf_op jit(solution)/shard_map/all_to_all | solution.py:98
  643.7 17.6 %fusion.188 = f32[12,1024]{1,0:T(8,128)S(1)} fusion(f32[1024,12]{0,1:T(8,128)S(1)} %squeeze.72, f32[1024]{0:T(1024)S(1)} %get-tuple-element.38, f32[1024]{0:T(1024)S(1)} %get-tuple-element.39, s32[12]{0:T(128)S(1)} %get-tuple-element.14, s32[12]{0:T(128)S(1)} %get-tuple-element.15), kind=kOutput, calls=%fused_computation.103 | convolution fusion | flops 165748736 | bytes 106592 | tf_op jit(solution)/shard_map/dot_general | solution.py:28
  661.3 20.9 %fusion.200 = bf16[1,1024,12]{1,2,0:T(8,128)(2,1)S(1)} fusion(f32[12,1024]{1,0:T(8,128)S(1)} %fusion.188), kind=kOutput, calls=%fused_computation.107 | convolution fusion | flops 165687296 | bytes 73728 | tf_op jit(solution)/shard_map/dot_general | solution.py:48
  682.4 17.7 %fusion.194 = f32[12,1024]{1,0:T(8,128)S(1)} fusion(f32[1024,12]{0,1:T(8,128)S(1)} %squeeze.73, f32[1024]{0:T(1024)S(1)} %get-tuple-element.38, f32[1024]{0:T(1024)S(1)} %get-tuple-element.39, s32[12]{0:T(128)S(1)} %get-tuple-element.14, s32[12]{0:T(128)S(1)} %get-tuple-element.15), kind=kOutput, calls=%fused_computation.105 | convolution fusion | flops 165761024 | bytes 106592 | tf_op jit(solution)/shard_map/dot_general | solution.py:35
  700.1 21.2 %fusion.209 = bf16[1,1024,12]{1,2,0:T(8,128)(2,1)S(1)} fusion(f32[12,1024]{1,0:T(8,128)S(1)} %fusion.194), kind=kOutput, calls=%fused_computation.110 | convolution fusion | flops 165699584 | bytes 73728 | tf_op jit(solution)/shard_map/dot_general | solution.py:55
  722.6 12.3 %all_to_all.118 = bf16[32,2,384]{2,1,0:T(2,128)(2,1)S(1)} all-to-all(bf16[32,2,384]{2,1,0:T(2,128)(2,1)S(1)} %reshape.125), channel_id=1, replica_groups=mesh['freq'=32,'rcv'=8] {'freq'}, dimensions={0} | all-to-all | bytes 98304 | tf_op jit(solution)/shard_map/all_to_all | solution.py:100
  752.9 7.4 copy.210
  760.3 6.7 stack.103
  767.0 5.9 pad_maximum_fusion.1
  772.9 8.1 copy.211
  781.0 9.3 reshape.127
  790.3 43.0 %all_to_all.119 = bf16[32,2,12288]{2,1,0:T(2,128)(2,1)S(1)} all-to-all(bf16[32,2,12288]{2,1,0:T(2,128)(2,1)S(1)} %reshape.127), channel_id=1, replica_groups=mesh['freq'=32,'rcv'=8] {'freq'}, dimensions={0} | all-to-all | bytes 3145728 | tf_op jit(solution)/shard_map/all_to_all | solution.py:118
  843.2 9.1 copy.212
  852.3 9.7 all_to_all.104
  862.0 96.2 %all-reduce.7.cloned.1.call-done = bf16[2,1024,8,1,48]{1,4,3,2,0:T(8,128)(2,1)} async-done(((bf16[2,1024,8,1,48]{1,4,3,2,0:T(8,128)(2,1)}), bf16[2,1024,8,1,48]{1,4,3,2,0:T(8,128)(2,1)}) %all-reduce.7.cloned.1.call-update) | async-done | bytes 1572880
  959.9 18.2 %fusion.128 = f32[48,1024]{1,0:T(8,128)S(1)} fusion(f32[2,1024,1,1,48]{1,4,3,2,0:T(8,128)S(1)} %dynamic-slice_convert_fusion, f32[1024]{0:T(1024)S(1)} %get-tuple-element.38, f32[1024]{0:T(1024)S(1)} %get-tuple-element.39, s32[48]{0:T(128)S(1)} %copy-done.11, s32[48]{0:T(128)S(1)} %copy-done.13), kind=kOutput, calls=%fused_computation.83 | convolution fusion | flops 619003904 | bytes 402432 | tf_op jit(solution)/shard_map/dot_general | solution.py:35
  978.1 18.3 %fusion.134 = f32[48,1024]{1,0:T(8,128)S(1)} fusion(f32[2,1024,1,1,48]{1,4,3,2,0:T(8,128)S(1)} %dynamic-slice_convert_fusion, f32[1024]{0:T(1024)S(1)} %get-tuple-element.38, f32[1024]{0:T(1024)S(1)} %get-tuple-element.39, s32[48]{0:T(128)S(1)} %copy-done.11, s32[48]{0:T(128)S(1)} %copy-done.13), kind=kOutput, calls=%fused_computation.85 | convolution fusion | flops 618954752 | bytes 402432 | tf_op jit(solution)/shard_map/dot_general | solution.py:28
  996.4 21.5 %fusion.140 = bf16[1,1024,48]{1,2,0:T(8,128)(2,1)S(1)} fusion(f32[48,1024]{1,0:T(8,128)S(1)} %fusion.134), kind=kOutput, calls=%fused_computation.87 | convolution fusion | flops 618708992 | bytes 294912 | tf_op jit(solution)/shard_map/dot_general | solution.py:48
  1017.9 21.6 %fusion.149 = bf16[1,1024,48]{1,2,0:T(8,128)(2,1)S(1)} fusion(f32[48,1024]{1,0:T(8,128)S(1)} %fusion.128), kind=kOutput, calls=%fused_computation.90 | convolution fusion | flops 618758144 | bytes 294912 | tf_op jit(solution)/shard_map/dot_general | solution.py:55
  1041.4 10.8 %all-to-all-start.7 = ((bf16[32,2,1536]{2,1,0:T(2,128)(2,1)}), bf16[32,2,1536]{2,1,0:T(2,128)(2,1)S(1)}, u32[]{:S(2)}, u32[]{:S(2)}) async-start(bf16[32,2,1536]{2,1,0:T(2,128)(2,1)} %reshape.129), calls=%async_computation.7 | async-start | bytes 393216 | tf_op jit(solution)/shard_map/all_to_all | solution.py:126
  1053.3 9.1 all-to-all-done.7
  (142 shorter events, 121.0 us)
Async XLA Ops:
  7.2 62.6 %all-gather.3.cloned.1.call-start = ((), (), s32[]{:S(2)}) async-start(), calls=%async_computation.8 | async-start | bytes 1769472 | tf_op jit(solution)/shard_map/all_gather | solution.py:83
  89.8 5.3 copy-start.7
  95.2 2.8 copy-start
  100.7 17.9 %all-to-all-start = ((f32[32,1,768]{2,1,0:T(1,128)}), f32[32,1,768]{2,1,0:T(1,128)S(1)}, u32[]{:S(2)}, u32[]{:S(2)}) async-start(f32[32,1,768]{2,1,0:T(1,128)} %reshape.115), calls=%async_computation | async-start | bytes 196608 | tf_op jit(solution)/shard_map/all_to_all | solution.py:98
  110.2 325.4 %all-reduce.5.cloned.1.call-start = ((), (), s32[]{:S(2)}) async-start(), calls=%async_computation.10 | async-start | bytes 3145728
  214.6 2.8 copy-start.1
  329.6 9.8 copy-start.9
  329.6 10.0 copy-start.14
  339.3 254.2 %all-gather.5.cloned.1.call-start = ((), (), s32[]{:S(2)}) async-start(), calls=%async_computation.9 | async-start | bytes 1769472 | tf_op jit(solution)/shard_map/all_gather | solution.py:83
  340.3 136.6 %copy-start.10 = (s32[48]{0:T(128)}, s32[48]{0:T(128)S(1)}, u32[]{:S(2)}) copy-start(s32[48]{0:T(128)S(1)} %get-tuple-element.12) | copy-start | bytes 580
  340.3 136.6 %copy-start.12 = (s32[48]{0:T(128)}, s32[48]{0:T(128)S(1)}, u32[]{:S(2)}) copy-start(s32[48]{0:T(128)S(1)} %get-tuple-element.13) | copy-start | bytes 580
  517.4 24.9 %copy-start.4 = (f32[2,32,1536]{2,1,0:T(8,128)S(1)}, f32[2,32,1536]{2,1,0:T(8,128)}, u32[]{:S(2)}) copy-start(f32[2,32,1536]{2,1,0:T(8,128)} %param.5) | copy-start | bytes 1179652
  543.0 415.2 %all-reduce.7.cloned.1.call-start = ((), (), s32[]{:S(2)}) async-start(), calls=%async_computation.11 | async-start | bytes 3145728
  613.7 5.3 copy-start.8
  619.0 2.8 copy-start.2
  737.0 2.4 copy-start.5
  737.0 2.9 copy-start.3
  852.3 107.5 %copy-start.11 = (s32[48]{0:T(128)S(1)}, s32[48]{0:T(128)}, u32[]{:S(2)}) copy-start(s32[48]{0:T(128)} %copy-done.10) | copy-start | bytes 580
  852.3 107.5 %copy-start.13 = (s32[48]{0:T(128)S(1)}, s32[48]{0:T(128)}, u32[]{:S(2)}) copy-start(s32[48]{0:T(128)} %copy-done.12) | copy-start | bytes 580
  1017.9 34.3 %copy-start.6 = (bf16[2,32,32,12]{1,2,3,0:T(8,128)(2,1)S(1)}, bf16[2,32,32,12]{1,2,3,0:T(8,128)(2,1)}, u32[]{:S(2)}) copy-start(bf16[2,32,32,12]{1,2,3,0:T(8,128)(2,1)} %copy-done.5) | copy-start | bytes 147460
  1041.4 21.0 %all-to-all-start.7 = ((bf16[32,2,1536]{2,1,0:T(2,128)(2,1)}), bf16[32,2,1536]{2,1,0:T(2,128)(2,1)S(1)}, u32[]{:S(2)}, u32[]{:S(2)}) async-start(bf16[32,2,1536]{2,1,0:T(2,128)(2,1)} %reshape.129), calls=%async_computation.7 | async-start | bytes 393216 | tf_op jit(solution)/shard_map/all_to_all | solution.py:126
Sparse Core Ops, SparseCore 0:
  11.2 58.4 all-gather.2
  339.5 96.1 all-reduce.4
  543.1 50.3 all-gather.4
  862.1 96.0 all-reduce.6
where the time goes:
time: 1080 us; the launch traced here: 1070 us
  matrix products  326 us (30%)
  waiting for transfers between devices  319 us (30%)
  local copies, waits for them, and re-layouts  218 us (20%)
  blocking collectives  149 us (14%)
  other arithmetic  24.9 us (2%)
  starting transfers between devices  20.4 us (2%)
  between operations  15.1 us (1%)
    unnamed x6, waiting for transfers between devices  192 us
    all_gather x2, waiting for transfers between devices, local(): gathered = lax.all_gather(plus_half, 'rcv', axis=2, tiled=True)  110 us
    all_to_all x2, blocking collectives, local(): lax.all_to_all(blocks.astype(jnp.bfloat16), 'freq', split_axis=3, concat_...  85.7 us
    dot_general x4, matrix products, window_traces(): lax.dot_general(sines, odd_part, back, precision=lax.Precision.HIGHEST, p...  85.3 us
    dot_general x4, matrix products, window_traces(): lax.dot_general(cosines, even_part, back, precision=lax.Precision.HIGHEST...  84.7 us
    dot_general x4, matrix products, window_traces(): lax.dot_general(spectrum[0] * weights, cosines, numbers, precision=lax.Pr...  71.9 us
    dot_general x4, matrix products, window_traces(): lax.dot_general(spectrum[1] * weights, sines, numbers, precision=lax.Prec...  71.8 us
    all_to_all x6, local copies, waits for them, and re-layouts, local(): lax.all_to_all(blocks.astype(jnp.bfloat16), 'freq', split_axis=3, concat_...  47 us
  transfers between devices with their start and end apart: 6, of which 6 were waited for; matrix products, arithmetic and copies ran while one was open for 0% of the time, Pallas kernels for 0%

commit v1 on v0

v1 whole, which is shorter than its diff:
```python
import math

import jax
import jax.numpy as jnp
import numpy as np
from jax import lax
from jax.experimental import pallas as pl
from jax.experimental.pallas import tpu as pltpu
from jax.sharding import PartitionSpec as P

MESH = pl.DeviceIdType.MESH
PS = 12
ITERS = 2
FB = 32
NB = 32
NR = 8
GF = 8
NG = FB // GF
ROWS = 2 * PS * GF
ML = 32
SL = 128
NK = FB * NB
TW = 768
NQ = 3
WM = 2 * NQ
WP = 2 * PS
F32 = jnp.float32
BF16 = jnp.bfloat16


def tables():
    index = np.arange(NK)
    phases = (index[:, None] * index[None, :]) % (2 * NK)
    angles = phases * (2.0 * math.pi / (2 * NK))
    return np.stack([np.cos(angles), np.sin(angles)]).astype(np.float32)


def reorder_rows(start, rows, count):
    index = start + lax.broadcasted_iota(jnp.int32, (rows, 1), 0)
    item = (index * 43691) >> 19
    target = (index - PS * item) * count + item
    lane = lax.broadcasted_iota(jnp.int32, (rows, PS * count), 1)
    return jnp.where(lane == target, 1.0, 0.0).astype(BF16)


def spreading():
    row = lax.broadcasted_iota(jnp.int32, (4 * ML, 4 * GF * ML), 0)
    lane = lax.broadcasted_iota(jnp.int32, (4 * ML, 4 * GF * ML), 1)
    hit = (lane // (GF * ML) == row // ML) & (lax.rem(lane, ML) == lax.rem(row, ML))
    return jnp.where(hit, 1.0, 0.0).astype(BF16)


MINUS_AT = (0, 10, 20, 5, 26, 30)


def minus_device(w):
    at = jnp.int32(MINUS_AT[0])
    for role in range(1, WM):
        at = jnp.where(w == role, MINUS_AT[role], at)
    return at


def plus_device(w):
    return jnp.where(w < 16, 2 * w, 4 * (w - 16) + 1)


def kernel(
    refl_hbm, tab_hbm, plus_ref, onm_ref, onp_ref,
    out_minus, out_plus,
    refl, tab_full, tab, perm, perm_m, spread, pinit, psnd, gath, mraw, msnd, xm, ymsnd, ym, spread_out, psum_snd, psum_rcv, total,
    xsnd, xp, ypsnd, wp, eo,
    load_sem, gath_send, gath_recv, xm_send, xm_recv, ym_send, ym_recv, rs_send, rs_recv, xp_send, xp_recv,
    wp_send, wp_recv,
):
    me_f = lax.axis_index("freq")
    me_r = lax.axis_index("rcv")

    chip = me_f // 2
    core = lax.rem(me_f, 2)
    w_minus = jnp.int32(0)
    is_minus = me_f == MINUS_AT[0]
    for role in range(1, WM):
        w_minus = jnp.where(me_f == MINUS_AT[role], role, w_minus)
        is_minus = is_minus | (me_f == MINUS_AT[role])
    w_plus = jnp.where(core == 0, chip, 16 + chip // 2)
    is_plus = (core == 0) | (lax.rem(chip, 2) == 0)
    part = jnp.minimum(w_plus, WP - 1) // PS

    load_refl = pltpu.make_async_copy(refl_hbm, refl, load_sem.at[0])
    load_tab = pltpu.make_async_copy(tab_hbm.at[part], tab_full, load_sem.at[1])
    load_refl.start()
    load_tab.start()

    barrier = pltpu.get_barrier_semaphore()

    def greet_f(i, _):
        pl.semaphore_signal(
            barrier, inc=1, device_id={"freq": lax.rem(me_f + i, NB), "rcv": me_r}, device_id_type=MESH
        )
        return 0

    def greet_r(i, _):
        pl.semaphore_signal(
            barrier, inc=1, device_id={"freq": me_f, "rcv": lax.rem(me_r + i, NR)}, device_id_type=MESH
        )
        return 0

    lax.fori_loop(1, NB, greet_f, 0)
    lax.fori_loop(1, NR, greet_r, 0)

    row32 = lax.broadcasted_iota(jnp.int32, (FB, 128), 0)
    k_scale = jnp.where((row32 == 0) & (me_f == 0), 0.5, 1.0).astype(F32)

    def remote_f(src, dst, send, recv, to):
        return pltpu.make_async_remote_copy(
            src_ref=src, dst_ref=dst, send_sem=send, recv_sem=recv,
            device_id={"freq": to, "rcv": me_r}, device_id_type=MESH,
        )

    def remote_r(src, dst, send, recv, to):
        return pltpu.make_async_remote_copy(
            src_ref=src, dst_ref=dst, send_sem=send, recv_sem=recv,
            device_id={"freq": me_f, "rcv": to}, device_id_type=MESH,
        )

    def await_bytes(ref, sem):
        pltpu.make_async_copy(ref, ref, sem).wait()

    def send_plus(it, g):
        rows = pl.ds(pl.multiple_of(g * ROWS, ROWS), ROWS)
        gath[it, me_r, rows, :] = psnd[it, rows, :]

        def one(i, _):
            to = lax.rem(me_r + i, NR)
            remote_r(
                psnd.at[it, rows], gath.at[it, me_r, rows], gath_send.at[it], gath_recv.at[it, g], to
            ).start()
            return 0

        lax.fori_loop(1, NR, one, 0)

    def fill_perm(i, _):
        perm[pl.ds(pl.multiple_of(i * 128, 128), 128), :] = reorder_rows(i * 128, 128, SL)
        return 0

    lax.fori_loop(0, PS, fill_perm, 0)
    first = jnp.dot(plus_ref[...].astype(BF16), perm[...], preferred_element_type=F32)
    pl.semaphore_wait(barrier, NB - 1 + NR - 1)
    for g in range(NG):
        parts = [
            first[c * FB + g * GF : c * FB + (g + 1) * GF, p * SL : (p + 1) * SL]
            for c in range(2)
            for p in range(PS)
        ]
        psnd[0, g * ROWS : (g + 1) * ROWS, :] = jnp.concatenate(parts, axis=0).astype(BF16)
        send_plus(0, g)

    left = plus_ref[...] - plus_ref[...].astype(BF16).astype(F32)
    middle = left.astype(BF16)
    small = (left - middle.astype(F32)).astype(BF16)
    rest = jnp.dot(jnp.concatenate([middle, small], axis=0), perm[...], preferred_element_type=F32)
    exact = first + (rest[: 2 * FB] + rest[2 * FB :])
    for c in range(2):
        for p in range(PS):
            pinit[c * PS + p] = exact[c * FB : (c + 1) * FB, p * SL : (p + 1) * SL]

    spread[...] = spreading()
    perm_m[...] = reorder_rows(0, ML * PS, ML)
    load_tab.wait()

    def split_tab(i, _):
        rows = pl.ds(pl.multiple_of(i * 128, 128), 128)
        values = tab_full[rows, :]
        high = values.astype(BF16)
        tab[0, rows, :] = high
        tab[1, rows, :] = (values - high.astype(F32)).astype(BF16)
        return 0

    lax.fori_loop(0, NK // 128, split_tab, 0)
    load_refl.wait()

    def window(x, onsets, y, send_rows):
        step_t = 256

        def forward(i, _):
            rows = pl.ds(pl.multiple_of(i * step_t, step_t), step_t)
            values = x[...]
            in_time = jnp.dot(tab[0, rows, :], values, preferred_element_type=F32)
            in_time += jnp.dot(tab[1, rows, :], values, preferred_element_type=F32)
            time = i * step_t + lax.broadcasted_iota(jnp.int32, (step_t, 128), 0)
            factor = jnp.where(time == 0, 1.0 / NK, 2.0 / NK).astype(F32)
            in_time = jnp.where(time < onsets, in_time * factor, 0.0)
            high = in_time.astype(BF16)
            eo[rows, :128] = high
            eo[rows, 128:] = (in_time - high.astype(F32)).astype(BF16)
            return 0

        lax.fori_loop(0, TW // step_t, forward, 0)

        def back(i, _):
            rows = pl.ds(pl.multiple_of(i * step_t, step_t), step_t)
            both = jnp.dot(tab[0, rows, :TW], eo[...], preferred_element_type=F32)
            small = jnp.dot(tab[1, rows, :TW], eo[:, :128], preferred_element_type=F32)
            y[rows, :] = (both[:, :128] + (both[:, 128:] + small)).astype(BF16)
            send_rows(i, step_t // FB)
            return 0

        lax.fori_loop(0, NK // step_t, back, 0)

    def iteration(it, _):
        lane = lax.broadcasted_iota(jnp.int32, (ROWS // 2, 256), 1)
        row = lax.broadcasted_iota(jnp.int32, (ROWS // 2, 256), 0)
        same = lax.rem(row, GF) == lane // ML
        quad_lane = lax.broadcasted_iota(jnp.int32, (GF, 128), 1) // ML

        def forward(g, _):
            await_bytes(gath.at[it, pl.ds(0, NR - 1), pl.ds(0, ROWS)], gath_recv.at[it, g])
            rows = pl.ds(pl.multiple_of(g * ROWS, ROWS), ROWS)
            values = jnp.concatenate([gath[it, r, rows, :] for r in range(NR)], axis=1)
            dims = (((1,), (1,)), ((), ()))
            rows_re = pl.ds(pl.multiple_of(g * (GF * ML), GF * ML), GF * ML)
            rows_im = pl.ds(pl.multiple_of(FB * ML + g * (GF * ML), GF * ML), GF * ML)
            a = lax.dot_general(values, refl[rows_re, :], dims, preferred_element_type=F32)
            b = lax.dot_general(values, refl[rows_im, :], dims, preferred_element_type=F32)
            half = ROWS // 2
            parts = (a[:half] - b[half:], b[:half] + a[half:])
            for c in range(2):
                own = jnp.where(same, parts[c], 0.0)
                own = own[:, :128] + own[:, 128:]
                own = own + pltpu.roll(own, 64, 1)
                own = own + pltpu.roll(own, 32, 1)
                for q in range(NQ):
                    block = jnp.zeros((GF, 128), F32)
                    for i in range(4):
                        p = 4 * q + i
                        block = jnp.where(quad_lane == i, own[p * GF : (p + 1) * GF], block)
                    mraw[c * NQ + q, pl.ds(pl.multiple_of(g * GF, GF), GF), :] = block
            return 0

        lax.fori_loop(0, NG, forward, 0)

        my_rows = pl.ds(pl.multiple_of(me_f * FB, FB), FB)

        def send_minus(w, _):
            to = minus_device(w)
            msnd[it, w] = (mraw[w] * k_scale).astype(BF16)

            @pl.when(to == me_f)
            def _():
                xm[it, my_rows, :] = msnd[it, w]

            @pl.when(to != me_f)
            def _():
                remote_f(
                    msnd.at[it, w], xm.at[it, my_rows], xm_send.at[it], xm_recv.at[it], to
                ).start()

            return 0

        lax.fori_loop(0, WM, send_minus, 0)

        @pl.when(is_minus)
        def _():
            await_bytes(xm.at[it, pl.ds(0, NK - FB)], xm_recv.at[it])
            onsets = onm_ref[pl.ds(lax.rem(w_minus, NQ), 1), :]

            def send_rows(chunk, count):
                def one(i, _):
                    to = chunk * count + i
                    rows = pl.ds(pl.multiple_of(to * FB, FB), FB)

                    @pl.when(to == me_f)
                    def _():
                        ym[it, w_minus] = ymsnd[it, rows, :]

                    @pl.when(to != me_f)
                    def _():
                        remote_f(
                            ymsnd.at[it, rows], ym.at[it, w_minus], ym_send.at[it], ym_recv.at[it], to
                        ).start()

                    return 0

                lax.fori_loop(0, count, one, 0)

            window(xm.at[it], onsets, ymsnd.at[it], send_rows)

        @pl.when(is_minus)
        def _():
            await_bytes(ym.at[it, pl.ds(0, WM - 1)], ym_recv.at[it])

        @pl.when(jnp.logical_not(is_minus))
        def _():
            await_bytes(ym.at[it], ym_recv.at[it])

        wide = jnp.dot(ym[it].reshape(WM * FB, 128), spread[...], preferred_element_type=F32)
        row_s = lax.broadcasted_iota(jnp.int32, (WM * FB, 1024), 0)
        lane_s = lax.broadcasted_iota(jnp.int32, (WM * FB, 1024), 1)
        wide = jnp.where(lax.rem(row_s, GF) == lax.rem(lane_s // ML, GF), wide, 0.0)
        spread_out[...] = wide.reshape(WM, FB, 1024)

        def adjoint(g, _):
            frows = pl.ds(pl.multiple_of(g * GF, GF), GF)
            blocks = [spread_out[w, frows, :] for w in range(WM)]
            re = jnp.concatenate(
                [blocks[p // 4][:, (p % 4) * 256 : (p % 4 + 1) * 256] for p in range(PS)], axis=0
            )
            im = jnp.concatenate(
                [blocks[NQ + p // 4][:, (p % 4) * 256 : (p % 4 + 1) * 256] for p in range(PS)], axis=0
            )
            left = jnp.concatenate([re, im], axis=0).astype(BF16)
            right = jnp.concatenate([im, -re], axis=0).astype(BF16)
            rows_re = pl.ds(pl.multiple_of(g * (GF * ML), GF * ML), GF * ML)
            rows_im = pl.ds(pl.multiple_of(FB * ML + g * (GF * ML), GF * ML), GF * ML)
            rows = pl.ds(pl.multiple_of(g * ROWS, ROWS), ROWS)
            for n in range(4):
                cols = slice(n * 256, (n + 1) * 256)
                out = jnp.dot(left, refl[rows_re, cols], preferred_element_type=F32)
                out += jnp.dot(right, refl[rows_im, cols], preferred_element_type=F32)
                out = out.astype(BF16)
                psum_snd[it, 2 * n, rows, :] = out[:, :128]
                psum_snd[it, 2 * n + 1, rows, :] = out[:, 128:]
            psum_rcv[it, me_r, rows, :] = psum_snd[it, me_r, rows, :]

            def one(i, _):
                to = lax.rem(me_r + i, NR)
                remote_r(
                    psum_snd.at[it, to, rows], psum_rcv.at[it, me_r, rows], rs_send.at[it], rs_recv.at[it, g], to
                ).start()
                return 0

            lax.fori_loop(1, NR, one, 0)
            return 0

        lax.fori_loop(0, NG, adjoint, 0)

        def add_up(g, _):
            await_bytes(psum_rcv.at[it, pl.ds(0, NR - 1), pl.ds(0, ROWS)], rs_recv.at[it, g])
            rows = pl.ds(pl.multiple_of(g * ROWS, ROWS), ROWS)
            acc = psum_rcv[it, 0, rows, :].astype(F32)
            for r in range(1, NR):
                acc += psum_rcv[it, r, rows, :].astype(F32)
            total[:, pl.ds(pl.multiple_of(g * GF, GF), GF), :] = acc.reshape(WP, GF, SL)
            return 0

        lax.fori_loop(0, NG, add_up, 0)

        def send_total(w, _):
            to = plus_device(w)
            xsnd[it, w] = (total[w] * k_scale).astype(BF16)

            @pl.when(to == me_f)
            def _():
                xp[it, my_rows, :] = xsnd[it, w]

            @pl.when(to != me_f)
            def _():
                remote_f(
                    xsnd.at[it, w], xp.at[it, my_rows], xp_send.at[it], xp_recv.at[it], to
                ).start()

            return 0

        lax.fori_loop(0, WP, send_total, 0)

        @pl.when(is_plus)
        def _():
            await_bytes(xp.at[it, pl.ds(0, NK - FB)], xp_recv.at[it])
            onsets = onp_ref[pl.ds(lax.rem(w_plus, PS), 1), :]

            def send_rows(chunk, count):
                def one(i, _):
                    to = chunk * count + i
                    rows = pl.ds(pl.multiple_of(to * FB, FB), FB)

                    @pl.when(to == me_f)
                    def _():
                        wp[it, w_plus] = ypsnd[it, rows, :]

                    @pl.when(to != me_f)
                    def _():
                        remote_f(
                            ypsnd.at[it, rows], wp.at[it, w_plus], wp_send.at[it], wp_recv.at[it], to
                        ).start()

                    return 0

                lax.fori_loop(0, count, one, 0)

            window(xp.at[it], onsets, ypsnd.at[it], send_rows)

        @pl.when(is_plus)
        def _():
            await_bytes(wp.at[it, pl.ds(0, WP - 1)], wp_recv.at[it])

        @pl.when(jnp.logical_not(is_plus))
        def _():
            await_bytes(wp.at[it], wp_recv.at[it])

        @pl.when(it < ITERS - 1)
        def _():
            def update(g, _):
                frows = pl.ds(pl.multiple_of(g * GF, GF), GF)
                rows = pl.ds(pl.multiple_of(g * ROWS, ROWS), ROWS)
                total[...] = wp[it].astype(F32)
                new = pinit[:, frows, :] + total[:, frows, :]
                psnd[it + 1, rows, :] = new.reshape(ROWS, SL).astype(BF16)
                send_plus(it + 1, g)
                return 0

            lax.fori_loop(0, NG, update, 0)

        return 0

    lax.fori_loop(0, ITERS, iteration, 0)

    last = ITERS - 1
    dims = (((1,), (1,)), ((), ()))
    minus = jnp.concatenate(
        [jnp.concatenate([ym[last, c * NQ + q] for q in range(NQ)], axis=1) for c in range(2)], axis=0
    )
    out_minus[...] = lax.dot_general(minus, perm_m[...], dims, preferred_element_type=F32)
    change = jnp.concatenate(
        [jnp.concatenate([wp[last, c * PS + p] for p in range(PS)], axis=1) for c in range(2)], axis=0
    )
    out_plus[...] = plus_ref[...] + lax.dot_general(change, perm[...], dims, preferred_element_type=F32)

    def drain(it, _):
        await_bytes(gath.at[it, pl.ds(0, NR - 1)], gath_send.at[it])
        await_bytes(gath.at[it, pl.ds(0, NR - 1)], rs_send.at[it])

        @pl.when(is_minus)
        def _():
            await_bytes(msnd.at[it, pl.ds(0, WM - 1)], xm_send.at[it])
            await_bytes(ymsnd.at[it, pl.ds(0, NK - FB)], ym_send.at[it])

        @pl.when(jnp.logical_not(is_minus))
        def _():
            await_bytes(msnd.at[it], xm_send.at[it])

        @pl.when(is_plus)
        def _():
            await_bytes(xsnd.at[it, pl.ds(0, WP - 1)], xp_send.at[it])
            await_bytes(ypsnd.at[it, pl.ds(0, NK - FB)], wp_send.at[it])

        @pl.when(jnp.logical_not(is_plus))
        def _():
            await_bytes(xsnd.at[it], xp_send.at[it])

        return 0

    lax.fori_loop(0, ITERS, drain, 0)


def local(reflection, plus_init, onset_receiver, onset_source):
    onm = jnp.transpose(onset_receiver).reshape(NQ, 4 * ML)
    onp = jnp.transpose(onset_source)
    vmem = pl.BlockSpec(memory_space=pltpu.VMEM)
    hbm = pl.BlockSpec(memory_space=pl.ANY)
    dma = pltpu.SemaphoreType.DMA
    out_minus, out_plus = pl.pallas_call(
        kernel,
        out_shape=(
            jax.ShapeDtypeStruct((2 * FB, ML * PS), F32),
            jax.ShapeDtypeStruct((2 * FB, SL * PS), F32),
        ),
        in_specs=[hbm, hbm, vmem, vmem, vmem],
        out_specs=(vmem, vmem),
        scratch_shapes=[
            pltpu.VMEM((2 * FB * ML, 1024), BF16),
            pltpu.VMEM((NK, NK), F32),
            pltpu.VMEM((2, NK, NK), BF16),
            pltpu.VMEM((SL * PS, SL * PS), BF16),
            pltpu.VMEM((ML * PS, ML * PS), BF16),
            pltpu.VMEM((4 * ML, 4 * GF * ML), BF16),
            pltpu.VMEM((WP, FB, SL), F32),
            pltpu.VMEM((ITERS, NG * ROWS, SL), BF16),
            pltpu.VMEM((ITERS, NR, NG * ROWS, SL), BF16),
            pltpu.VMEM((WM, FB, 128), F32),
            pltpu.VMEM((ITERS, WM, FB, 128), BF16),
            pltpu.VMEM((ITERS, NK, 128), BF16),
            pltpu.VMEM((ITERS, NK, 128), BF16),
            pltpu.VMEM((ITERS, WM, FB, 128), BF16),
            pltpu.VMEM((WM, FB, 1024), F32),
            pltpu.VMEM((ITERS, NR, NG * ROWS, SL), BF16),
            pltpu.VMEM((ITERS, NR, NG * ROWS, SL), BF16),
            pltpu.VMEM((WP, FB, SL), F32),
            pltpu.VMEM((ITERS, WP, FB, SL), BF16),
            pltpu.VMEM((ITERS, NK, SL), BF16),
            pltpu.VMEM((ITERS, NK, SL), BF16),
            pltpu.VMEM((ITERS, WP, FB, SL), BF16),
            pltpu.VMEM((TW, 256), BF16),
            dma((2,)),
            dma((ITERS,)), dma((ITERS, NG)),
            dma((ITERS,)), dma((ITERS,)),
            dma((ITERS,)), dma((ITERS,)),
            dma((ITERS,)), dma((ITERS, NG)),
            dma((ITERS,)), dma((ITERS,)),
            dma((ITERS,)), dma((ITERS,)),
        ],
        compiler_params=pltpu.CompilerParams(
            collective_id=0, has_side_effects=True, vmem_limit_bytes=56 * 1024 * 1024
        ),
    )(
        reflection.reshape(2 * FB * ML, 1024),
        jnp.asarray(tables()),
        plus_init.reshape(2 * FB, SL * PS),
        onm,
        onp,
    )
    return out_minus.reshape(2, FB, ML * PS), out_plus.reshape(2, FB, SL * PS)


def solution(mesh):
    return jax.shard_map(
        local,
        mesh=mesh,
        in_specs=(
            P(None, "freq", "rcv", None),
            P(None, "freq", "rcv"),
            P("rcv", None),
            P("rcv", None),
        ),
        out_specs=(P(None, "freq", "rcv"), P(None, "freq", "rcv")),
        check_vma=False,
    )
```

time: 1080 us -> 163 us (0.15)
  matrix products: 326 us -> 0 us
  waiting for transfers between devices: 319 us -> 0 us
  local copies, waits for them, and re-layouts: 218 us -> 4.66 us
  Pallas kernels: 0 us -> 155 us
  blocking collectives: 149 us -> 0 us
  other arithmetic: 24.9 us -> 0 us
  starting transfers between devices: 20.4 us -> 0 us
  between operations: 15.1 us -> 0.64 us
    dot_general x24 -> x0, matrix products: 326 us -> none  [the longest x4 85.3 us: window_traces(): lax.dot_general(sines, odd_part, back, precision=lax.Precision.HIGHEST, p...]
    unnamed x6 -> x0, waiting for transfers between devices: 192 us -> none
    pallas_call x0 -> x1, Pallas kernels: none -> 155 us  [local(): pl.pallas_call(kernel, out_shape=(jax.ShapeDtypeStruct((2 * FB, ML * PS),...]
    all_to_all x6 -> x0, blocking collectives: 149 us -> none  [the longest x2 85.7 us: local(): lax.all_to_all(blocks.astype(jnp.bfloat16), 'freq', split_axis=3, concat_...]
    all_gather x2 -> x0, waiting for transfers between devices: 110 us -> none  [local(): gathered = lax.all_gather(plus_half, 'rcv', axis=2, tiled=True)]
    another operation x20 -> x0, local copies, waits for them, and re-layouts: 67.9 us -> none  [the longest x6 39.9 us: local(): jnp.stack([first_back[..., :P_SIZE] + second_back[..., P_SIZE:], first_ba...]
    all_to_all x11 -> x0, local copies, waits for them, and re-layouts: 50 us -> none  [the longest x6 47 us: local(): lax.all_to_all(blocks.astype(jnp.bfloat16), 'freq', split_axis=3, concat_...]
    unnamed x50 -> x2, local copies, waits for them, and re-layouts: 42.6 us -> 3.31 us
  transfers between devices with their start and end apart: 6 -> 0, of which waited for: 6 -> 0; matrix products, arithmetic and copies ran while one was open for 0% -> 0% of each run, Pallas kernels for 0% -> 0%
where the time goes in v1:
time: 163 us; the launch traced here: 161 us
  Pallas kernels  155 us (95%)
  local copies, waits for them, and re-layouts  4.66 us (3%)
    pallas_call x1, Pallas kernels, local(): pl.pallas_call(kernel, out_shape=(jax.ShapeDtypeStruct((2 * FB, ML * PS),...  155 us
    unnamed x2, local copies, waits for them, and re-layouts  3.31 us

profile of v1, /device:TPU:1, one launch (start us, length us, event | category | flops | bytes accessed | tf_op | source)
XLA Modules:
  0.0 160.5 jit_solution(12976611209625779086)
XLA Ops:
  0.6 1.4 reshape.21.onm_ref
  2.0 155.2 %shard_map.68 = (f32[64,384]{1,0:T(8,128)}, f32[64,1536]{1,0:T(8,128)}) custom-call(bf16[2048,1024]{1,0:T(8,128)(2,1)} %bitcast.6, f32[2,1024,1024]{2,1,0:T(8,128)} %constant.2.clone.tab_hbm, f32[64,1536]{1,0:T(8,128)} %bitcast.7, s32[3,128]{1,0:T(4,128)} %reshape.21.onm_ref, s32[12,128]{1,0:T(8,128)} %bitcast.10), custom_call_target="tpu_custom_call" | custom-call | tf_op jit(solution)/shard_map/pallas_call | solution.py:461
  157.2 1.5 copy.9
  158.8 1.8 %copy.10 = f32[2,32,1536]{2,1,0:T(8,128)} copy(f32[2,32,1536]{2,1,0:T(8,128)} %bitcast.8) | data formatting | bytes 786432

commit v2 on v1

v2 whole, which is shorter than its diff:
```python
import math

import jax
import jax.numpy as jnp
import numpy as np
from jax import lax
from jax.experimental import pallas as pl
from jax.experimental.pallas import tpu as pltpu
from jax.sharding import PartitionSpec as P

MESH = pl.DeviceIdType.MESH
PS = 12
ITERS = 2
FB = 32
NB = 32
NR = 8
GF = 8
NG = FB // GF
ROWS = 2 * 4 * GF
ML = 32
SL = 128
NK = FB * NB
TW = 768
NQ = 3
WM = 2 * NQ
WP = 2 * PS
F32 = jnp.float32
BF16 = jnp.bfloat16


def tables():
    index = np.arange(NK)
    phases = (index[:, None] * index[None, :]) % (2 * NK)
    angles = phases * (2.0 * math.pi / (2 * NK))
    return np.stack([np.cos(angles), np.sin(angles)]).astype(np.float32)


def reorder_rows(start, rows, count):
    index = start + lax.broadcasted_iota(jnp.int32, (rows, 1), 0)
    item = (index * 43691) >> 19
    target = (index - PS * item) * count + item
    lane = lax.broadcasted_iota(jnp.int32, (rows, PS * count), 1)
    return jnp.where(lane == target, 1.0, 0.0).astype(BF16)


def spreading():
    row = lax.broadcasted_iota(jnp.int32, (4 * ML, 4 * GF * ML), 0)
    lane = lax.broadcasted_iota(jnp.int32, (4 * ML, 4 * GF * ML), 1)
    hit = (lane // (GF * ML) == row // ML) & (lax.rem(lane, ML) == lax.rem(row, ML))
    return jnp.where(hit, 1.0, 0.0).astype(BF16)


MINUS_AT = ((3, 11, 5), (25, 17, 31))
PLUS_AT = (
    (0, 4, 8, 12, 2, 6, 10, 14, 1, 7, 9, 15),
    (18, 22, 26, 30, 16, 20, 24, 28, 19, 21, 27, 29),
)


def kernel(
    refl_hbm, tab_hbm, plus_ref, onm_ref, onp_ref,
    out_minus, out_plus,
    refl, tab_full, tab, perm, perm_m, spread, pinit, psnd, gath, msnd, xm, ymsnd, ym, wide, psum_snd, psum_rcv,
    xsnd, xp, ypsnd, wp, eo,
    load_sem, gath_send, gath_recv, xm_send, xm_recv, ym_send, ym_recv, rs_send, rs_recv, xp_send, xp_recv,
    wp_send, wp_recv,
):
    me_f = lax.axis_index("freq")
    me_r = lax.axis_index("rcv")
    part = me_f // (NB // 2)

    load_refl = pltpu.make_async_copy(refl_hbm, refl, load_sem.at[0])
    load_tab = pltpu.make_async_copy(tab_hbm.at[part], tab_full, load_sem.at[1])
    load_refl.start()
    load_tab.start()

    barrier = pltpu.get_barrier_semaphore()

    def greet_f(i, _):
        pl.semaphore_signal(
            barrier, inc=1, device_id={"freq": lax.rem(me_f + i, NB), "rcv": me_r}, device_id_type=MESH
        )
        return 0

    def greet_r(i, _):
        pl.semaphore_signal(
            barrier, inc=1, device_id={"freq": me_f, "rcv": lax.rem(me_r + i, NR)}, device_id_type=MESH
        )
        return 0

    lax.fori_loop(1, NB, greet_f, 0)
    lax.fori_loop(1, NR, greet_r, 0)

    row32 = lax.broadcasted_iota(jnp.int32, (FB, 128), 0)
    k_scale = jnp.where((row32 == 0) & (me_f == 0), 0.5, 1.0).astype(F32)
    my_rows = pl.ds(pl.multiple_of(me_f * FB, FB), FB)

    def remote_f(src, dst, send, recv, to):
        return pltpu.make_async_remote_copy(
            src_ref=src, dst_ref=dst, send_sem=send, recv_sem=recv,
            device_id={"freq": to, "rcv": me_r}, device_id_type=MESH,
        )

    def remote_r(src, dst, send, recv, to):
        return pltpu.make_async_remote_copy(
            src_ref=src, dst_ref=dst, send_sem=send, recv_sem=recv,
            device_id={"freq": me_f, "rcv": to}, device_id_type=MESH,
        )

    def await_bytes(ref, sem):
        pltpu.make_async_copy(ref, ref, sem).wait()

    def any_of(places):
        found = me_f == places[0]
        for place in places[1:]:
            found = found | (me_f == place)
        return found

    def minus_places(q):
        return [MINUS_AT[c][q] for c in range(2)]

    def plus_places(q):
        return [PLUS_AT[c][4 * q + i] for c in range(2) for i in range(4)]

    def send_plus(it, q):
        gath[it, q, me_r] = psnd[it, q]

        def one(i, _):
            to = lax.rem(me_r + i, NR)
            remote_r(psnd.at[it, q], gath.at[it, q, me_r], gath_send.at[it], gath_recv.at[it, q], to).start()
            return 0

        lax.fori_loop(1, NR, one, 0)

    def fill_perm(i, _):
        perm[pl.ds(pl.multiple_of(i * 128, 128), 128), :] = reorder_rows(i * 128, 128, SL)
        return 0

    lax.fori_loop(0, PS, fill_perm, 0)
    high = plus_ref[...].astype(BF16)
    left = plus_ref[...] - high.astype(F32)
    middle = left.astype(BF16)
    small = (left - middle.astype(F32)).astype(BF16)
    split = jnp.dot(jnp.concatenate([high, middle, small], axis=0), perm[...], preferred_element_type=F32)
    first = split[: 2 * FB]
    for q in range(NQ):
        for g in range(NG):
            parts = [
                first[c * FB + g * GF : c * FB + (g + 1) * GF, p * SL : (p + 1) * SL]
                for c in range(2)
                for p in range(4 * q, 4 * q + 4)
            ]
            psnd[0, q, g * ROWS : (g + 1) * ROWS, :] = jnp.concatenate(parts, axis=0).astype(BF16)
    pl.semaphore_wait(barrier, NB - 1 + NR - 1)
    for q in range(NQ):
        send_plus(0, q)

    exact = first + (split[2 * FB : 4 * FB] + split[4 * FB :])
    for c in range(2):
        for p in range(PS):
            pinit[p // 4, c * 4 + p % 4] = exact[c * FB : (c + 1) * FB, p * SL : (p + 1) * SL]

    spread[...] = spreading()
    perm_m[...] = reorder_rows(0, ML * PS, ML)
    load_tab.wait()

    def split_tab(i, _):
        rows = pl.ds(pl.multiple_of(i * 128, 128), 128)
        values = tab_full[rows, :]
        top = values.astype(BF16)
        tab[0, rows, :] = top
        tab[1, rows, :] = (values - top.astype(F32)).astype(BF16)
        return 0

    lax.fori_loop(0, NK // 128, split_tab, 0)
    load_refl.wait()

    def window(x, onsets, y, send_chunk):
        until = jnp.transpose(jnp.broadcast_to(onsets, (128, 128)))
        until = jnp.concatenate([until, until], axis=1)
        traces = jnp.transpose(x[...])
        for n in range(TW // 256):
            cols = slice(n * 256, (n + 1) * 256)
            in_time = jnp.dot(traces, tab[0, :, cols], preferred_element_type=F32)
            in_time += jnp.dot(traces, tab[1, :, cols], preferred_element_type=F32)
            time = n * 256 + lax.broadcasted_iota(jnp.int32, (128, 256), 1)
            factor = jnp.where(time == 0, 1.0 / NK, 2.0 / NK).astype(F32)
            in_time = jnp.where(time < until, in_time * factor, 0.0)
            top = in_time.astype(BF16)
            eo[:128, cols] = top
            eo[128:, cols] = (in_time - top.astype(F32)).astype(BF16)
        for n in range(NK // 256):
            cols = slice(n * 256, (n + 1) * 256)
            both = jnp.dot(eo[...], tab[0, :TW, cols], preferred_element_type=F32)
            small = jnp.dot(eo[:128, :], tab[1, :TW, cols], preferred_element_type=F32)
            y[cols, :] = jnp.transpose(both[:128] + (both[128:] + small)).astype(BF16)
            send_chunk(n * (256 // FB), 256 // FB)

    half = ROWS // 2
    lane = lax.broadcasted_iota(jnp.int32, (half, GF * ML), 1)
    row = lax.broadcasted_iota(jnp.int32, (half, GF * ML), 0)
    same = lax.rem(row, GF) == lane // ML
    quad_lane = lax.broadcasted_iota(jnp.int32, (GF, 128), 1) // ML

    def refl_rows(c, g):
        return slice(c * FB * ML + g * GF * ML, c * FB * ML + (g + 1) * GF * ML)

    def forward(it, q):
        await_bytes(gath.at[it, q, pl.ds(0, NR - 1)], gath_recv.at[it, q])
        dims = (((1,), (1,)), ((), ()))
        blocks = ([], [])
        for g in range(NG):
            rows = slice(g * ROWS, (g + 1) * ROWS)
            values = jnp.concatenate([gath[it, q, r, rows, :] for r in range(NR)], axis=1)
            a = lax.dot_general(values, refl[refl_rows(0, g), :], dims, preferred_element_type=F32)
            b = lax.dot_general(values, refl[refl_rows(1, g), :], dims, preferred_element_type=F32)
            parts = (a[:half] - b[half:], b[:half] + a[half:])
            for c in range(2):
                own = jnp.where(same, parts[c], 0.0)
                own = own[:, :128] + own[:, 128:]
                own = own + pltpu.roll(own, 64, 1)
                own = own + pltpu.roll(own, 32, 1)
                block = jnp.zeros((GF, 128), F32)
                for i in range(4):
                    block = jnp.where(quad_lane == i, own[i * GF : (i + 1) * GF], block)
                blocks[c].append(block)
        for c in range(2):
            to = MINUS_AT[c][q]
            msnd[it, q, c] = (jnp.concatenate(blocks[c], axis=0) * k_scale).astype(BF16)

            @pl.when(me_f == to)
            def _():
                xm[it, my_rows, :] = msnd[it, q, c]

            @pl.when(me_f != to)
            def _():
                remote_f(msnd.at[it, q, c], xm.at[it, my_rows], xm_send.at[it], xm_recv.at[it], to).start()

    def scatter(it, buffer, dst, send, recv):
        def send_chunk(begin, count):
            def one(i, _):
                to = begin + i
                rows = pl.ds(pl.multiple_of(to * FB, FB), FB)

                @pl.when(to == me_f)
                def _():
                    dst[...] = buffer[it, rows, :]

                @pl.when(to != me_f)
                def _():
                    remote_f(buffer.at[it, rows], dst, send, recv, to).start()

                return 0

            lax.fori_loop(0, count, one, 0)

        return send_chunk

    def window_minus(it, q):
        @pl.when(any_of(minus_places(q)))
        def _():
            await_bytes(xm.at[it, pl.ds(0, NK - FB)], xm_recv.at[it])
            onsets = jnp.concatenate([onm_ref[4 * q + i : 4 * q + i + 1, :] for i in range(4)], axis=1)
            send_chunk = scatter(it, ymsnd, ym.at[it, q, part], ym_send.at[it], ym_recv.at[it, q])
            window(xm.at[it], onsets, ymsnd.at[it], send_chunk)

    def adjoint(it, q):
        here = any_of(minus_places(q))

        @pl.when(here)
        def _():
            await_bytes(ym.at[it, q, pl.ds(0, 1)], ym_recv.at[it, q])

        @pl.when(jnp.logical_not(here))
        def _():
            await_bytes(ym.at[it, q], ym_recv.at[it, q])

        spread_rows = jnp.dot(ym[it, q].reshape(2 * FB, 128), spread[...], preferred_element_type=F32)
        row_s = lax.broadcasted_iota(jnp.int32, (2 * FB, 1024), 0)
        lane_s = lax.broadcasted_iota(jnp.int32, (2 * FB, 1024), 1)
        wide[...] = jnp.where(lax.rem(row_s, GF) == lax.rem(lane_s // ML, GF), spread_rows, 0.0)
        for g in range(NG):
            blocks = [wide[c * FB + g * GF : c * FB + (g + 1) * GF, :] for c in range(2)]
            re, im = [
                jnp.concatenate([block[:, i * 256 : (i + 1) * 256] for i in range(4)], axis=0) for block in blocks
            ]
            left = jnp.concatenate([re, im], axis=0).astype(BF16)
            right = jnp.concatenate([im, -re], axis=0).astype(BF16)
            for n in range(4):
                cols = slice(n * 256, (n + 1) * 256)
                out = jnp.dot(left, refl[refl_rows(0, g), cols], preferred_element_type=F32)
                out += jnp.dot(right, refl[refl_rows(1, g), cols], preferred_element_type=F32)
                out = out.astype(BF16)
                psum_snd[it, q, 2 * n, g * ROWS : (g + 1) * ROWS, :] = out[:, :128]
                psum_snd[it, q, 2 * n + 1, g * ROWS : (g + 1) * ROWS, :] = out[:, 128:]
        psum_rcv[it, q, me_r] = psum_snd[it, q, me_r]

        def one(i, _):
            to = lax.rem(me_r + i, NR)
            remote_r(
                psum_snd.at[it, q, to], psum_rcv.at[it, q, me_r], rs_send.at[it], rs_recv.at[it, q], to
            ).start()
            return 0

        lax.fori_loop(1, NR, one, 0)

    def add_up(it, q):
        await_bytes(psum_rcv.at[it, q, pl.ds(0, NR - 1)], rs_recv.at[it, q])
        total = psum_rcv[it, q, 0].astype(F32)
        for r in range(1, NR):
            total += psum_rcv[it, q, r].astype(F32)
        for c in range(2):
            for i in range(4):
                to = PLUS_AT[c][4 * q + i]
                at = c * 4 + i
                block = jnp.concatenate(
                    [total[g * ROWS + at * GF : g * ROWS + (at + 1) * GF] for g in range(NG)], axis=0
                )
                xsnd[it, q, at] = (block * k_scale).astype(BF16)

                @pl.when(me_f == to)
                def _():
                    xp[it, my_rows, :] = xsnd[it, q, at]

                @pl.when(me_f != to)
                def _():
                    remote_f(xsnd.at[it, q, at], xp.at[it, my_rows], xp_send.at[it], xp_recv.at[it], to).start()

    def window_plus(it, q):
        @pl.when(any_of(plus_places(q)))
        def _():
            await_bytes(xp.at[it, pl.ds(0, NK - FB)], xp_recv.at[it])
            point = jnp.int32(0)
            for i in range(1, 4):
                point = jnp.where(any_of([PLUS_AT[c][4 * q + i] for c in range(2)]), i, point)
            onsets = onp_ref[pl.ds(4 * q + point, 1), :]
            send_chunk = scatter(it, ypsnd, wp.at[it, q, part * 4 + point], wp_send.at[it], wp_recv.at[it, q])
            window(xp.at[it], onsets, ypsnd.at[it], send_chunk)

    def update(it, q):
        here = any_of(plus_places(q))

        @pl.when(here)
        def _():
            await_bytes(wp.at[it, q, pl.ds(0, 7)], wp_recv.at[it, q])

        @pl.when(jnp.logical_not(here))
        def _():
            await_bytes(wp.at[it, q], wp_recv.at[it, q])

        @pl.when(it < ITERS - 1)
        def _():
            new = pinit[q] + wp[it, q].astype(F32)
            for g in range(NG):
                rows = new[:, g * GF : (g + 1) * GF, :].reshape(ROWS, SL)
                psnd[it + 1, q, g * ROWS : (g + 1) * ROWS, :] = rows.astype(BF16)
            send_plus(it + 1, q)

        @pl.when(it == ITERS - 1)
        def _():
            change = jnp.concatenate(
                [jnp.concatenate([wp[it, q, c * 4 + i] for i in range(4)], axis=1) for c in range(2)], axis=0
            )
            dims = (((1,), (1,)), ((), ()))
            change = lax.dot_general(
                change, perm[:, q * 4 * SL : (q + 1) * 4 * SL], dims, preferred_element_type=F32
            )
            before = plus_ref if q == 0 else out_plus
            out_plus[...] = before[...] + change

    def finish_minus(it):
        @pl.when(it == ITERS - 1)
        def _():
            minus = jnp.concatenate(
                [jnp.concatenate([ym[it, q, c] for q in range(NQ)], axis=1) for c in range(2)], axis=0
            )
            dims = (((1,), (1,)), ((), ()))
            out_minus[...] = lax.dot_general(minus, perm_m[...], dims, preferred_element_type=F32)

    def iteration(it, _):
        forward(it, 0)
        window_minus(it, 0)
        forward(it, 1)
        window_minus(it, 1)
        forward(it, 2)
        adjoint(it, 0)
        window_minus(it, 2)
        adjoint(it, 1)
        adjoint(it, 2)
        add_up(it, 0)
        finish_minus(it)
        add_up(it, 1)
        window_plus(it, 0)
        add_up(it, 2)
        window_plus(it, 1)
        update(it, 0)
        window_plus(it, 2)
        update(it, 1)
        update(it, 2)
        return 0

    lax.fori_loop(0, ITERS, iteration, 0)

    is_minus = any_of([place for q in range(NQ) for place in minus_places(q)])
    is_plus = any_of([place for q in range(NQ) for place in plus_places(q)])

    def drain(it, _):
        await_bytes(gath.at[it, :, pl.ds(0, NR - 1)], gath_send.at[it])
        await_bytes(gath.at[it, :, pl.ds(0, NR - 1)], rs_send.at[it])

        @pl.when(is_minus)
        def _():
            await_bytes(xm.at[it, pl.ds(0, (WM - 1) * FB)], xm_send.at[it])
            await_bytes(ymsnd.at[it, pl.ds(0, NK - FB)], ym_send.at[it])

        @pl.when(jnp.logical_not(is_minus))
        def _():
            await_bytes(msnd.at[it], xm_send.at[it])

        @pl.when(is_plus)
        def _():
            await_bytes(xp.at[it, pl.ds(0, (WP - 1) * FB)], xp_send.at[it])
            await_bytes(ypsnd.at[it, pl.ds(0, NK - FB)], wp_send.at[it])

        @pl.when(jnp.logical_not(is_plus))
        def _():
            await_bytes(xsnd.at[it], xp_send.at[it])

        return 0

    lax.fori_loop(0, ITERS, drain, 0)


def local(reflection, plus_init, onset_receiver, onset_source):
    onm = jnp.transpose(onset_receiver)
    onp = jnp.transpose(onset_source)
    vmem = pl.BlockSpec(memory_space=pltpu.VMEM)
    hbm = pl.BlockSpec(memory_space=pl.ANY)
    dma = pltpu.SemaphoreType.DMA
    out_minus, out_plus = pl.pallas_call(
        kernel,
        out_shape=(
            jax.ShapeDtypeStruct((2 * FB, ML * PS), F32),
            jax.ShapeDtypeStruct((2 * FB, SL * PS), F32),
        ),
        in_specs=[hbm, hbm, vmem, vmem, vmem],
        out_specs=(vmem, vmem),
        scratch_shapes=[
            pltpu.VMEM((2 * FB * ML, 1024), BF16),
            pltpu.VMEM((NK, NK), F32),
            pltpu.VMEM((2, NK, NK), BF16),
            pltpu.VMEM((SL * PS, SL * PS), BF16),
            pltpu.VMEM((ML * PS, ML * PS), BF16),
            pltpu.VMEM((4 * ML, 4 * GF * ML), BF16),
            pltpu.VMEM((NQ, 8, FB, SL), F32),
            pltpu.VMEM((ITERS, NQ, NG * ROWS, SL), BF16),
            pltpu.VMEM((ITERS, NQ, NR, NG * ROWS, SL), BF16),
            pltpu.VMEM((ITERS, NQ, 2, FB, 128), BF16),
            pltpu.VMEM((ITERS, NK, 128), BF16),
            pltpu.VMEM((ITERS, NK, 128), BF16),
            pltpu.VMEM((ITERS, NQ, 2, FB, 128), BF16),
            pltpu.VMEM((2 * FB, 1024), F32),
            pltpu.VMEM((ITERS, NQ, NR, NG * ROWS, SL), BF16),
            pltpu.VMEM((ITERS, NQ, NR, NG * ROWS, SL), BF16),
            pltpu.VMEM((ITERS, NQ, 8, FB, SL), BF16),
            pltpu.VMEM((ITERS, NK, SL), BF16),
            pltpu.VMEM((ITERS, NK, SL), BF16),
            pltpu.VMEM((ITERS, NQ, 8, FB, SL), BF16),
            pltpu.VMEM((256, TW), BF16),
            dma((2,)),
            dma((ITERS,)), dma((ITERS, NQ)),
            dma((ITERS,)), dma((ITERS,)),
            dma((ITERS,)), dma((ITERS, NQ)),
            dma((ITERS,)), dma((ITERS, NQ)),
            dma((ITERS,)), dma((ITERS,)),
            dma((ITERS,)), dma((ITERS, NQ)),
        ],
        compiler_params=pltpu.CompilerParams(
            collective_id=0, has_side_effects=True, vmem_limit_bytes=56 * 1024 * 1024
        ),
    )(
        reflection.reshape(2 * FB * ML, 1024),
        jnp.asarray(tables()),
        plus_init.reshape(2 * FB, SL * PS),
        onm,
        onp,
    )
    return out_minus.reshape(2, FB, ML * PS), out_plus.reshape(2, FB, SL * PS)


def solution(mesh):
    return jax.shard_map(
        local,
        mesh=mesh,
        in_specs=(
            P(None, "freq", "rcv", None),
            P(None, "freq", "rcv"),
            P("rcv", None),
            P("rcv", None),
        ),
        out_specs=(P(None, "freq", "rcv"), P(None, "freq", "rcv")),
        check_vma=False,
    )
```

time: 163 us -> 147 us (0.902); the launches traced: 161 us -> 147 us
  Pallas kernels: 155 us -> 143 us
    pallas_call x1, Pallas kernels: 155 us -> 143 us  [local(): pl.pallas_call(kernel, out_shape=(jax.ShapeDtypeStruct((2 * FB, ML * PS),...]
where the time goes in v2:
time: 147 us
  Pallas kernels  143 us (97%)
  local copies, waits for them, and re-layouts  3.31 us (2%)
    pallas_call x1, Pallas kernels, local(): pl.pallas_call(kernel, out_shape=(jax.ShapeDtypeStruct((2 * FB, ML * PS),...  143 us
    unnamed x2, local copies, waits for them, and re-layouts  3.31 us

profile of v2, /device:TPU:1, one launch (start us, length us, event | category | flops | bytes accessed | tf_op | source)
XLA Modules:
  0.0 146.6 jit_solution(14941306436878898009)
XLA Ops:
  0.6 142.7 %shard_map.68 = (f32[64,384]{1,0:T(8,128)}, f32[64,1536]{1,0:T(8,128)}) custom-call(bf16[2048,1024]{1,0:T(8,128)(2,1)} %bitcast.6, f32[2,1024,1024]{2,1,0:T(8,128)} %constant.2.clone.tab_hbm, f32[64,1536]{1,0:T(8,128)} %bitcast.7, s32[12,32]{1,0:T(8,128)} %bitcast.10, s32[12,128]{1,0:T(8,128)} %bitcast.11), custom_call_target="tpu_custom_call" | custom-call | tf_op jit(solution)/shard_map/pallas_call | solution.py:440
  143.3 1.5 %copy.9 = f32[2,32,384]{2,1,0:T(8,128)} copy(f32[2,32,384]{2,1,0:T(8,128)} %bitcast.9) | data formatting | bytes 196608
  144.9 1.8 %copy.10 = f32[2,32,1536]{2,1,0:T(8,128)} copy(f32[2,32,1536]{2,1,0:T(8,128)} %bitcast.8) | data formatting | bytes 786432

commit v3 on v2

--- a/solution.py
+++ b/solution.py
@@ -14,9 +14,11 @@
 FB = 32
 NB = 32
 NR = 8
+NX = 4
 GF = 8
 NG = FB // GF
 ROWS = 2 * 4 * GF
+HALF = NG * ROWS // 2
 ML = 32
 SL = 128
 NK = FB * NB
@@ -60,14 +62,20 @@
 def kernel(
     refl_hbm, tab_hbm, plus_ref, onm_ref, onp_ref,
     out_minus, out_plus,
-    refl, tab_full, tab, perm, perm_m, spread, pinit, psnd, gath, msnd, xm, ymsnd, ym, wide, psum_snd, psum_rcv,
-    xsnd, xp, ypsnd, wp, eo,
+    refl, tab_full, tab, perm, perm_m, spread, pinit, psnd, gath, msnd, xm, ymsnd, ym, wide,
+    part_a, part_b, from_x, from_y, sum_a, sum_b, rest_a, rest_b, xsnd, xp, ypsnd, wp, eo,
     load_sem, gath_send, gath_recv, xm_send, xm_recv, ym_send, ym_recv, rs_send, rs_recv, xp_send, xp_recv,
     wp_send, wp_recv,
 ):
     me_f = lax.axis_index("freq")
     me_r = lax.axis_index("rcv")
     part = me_f // (NB // 2)
+    me_x, me_y = me_r // 2, lax.rem(me_r, 2)
+    beside = me_x * 2 + (1 - me_y)
+
+    def along_x(i):
+        return lax.rem(me_x + i, NX)
+
 
     load_refl = pltpu.make_async_copy(refl_hbm, refl, load_sem.at[0])
     load_tab = pltpu.make_async_copy(tab_hbm.at[part], tab_full, load_sem.at[1])
@@ -124,13 +132,20 @@
 
     def send_plus(it, q):
         gath[it, q, me_r] = psnd[it, q]
-
-        def one(i, _):
-            to = lax.rem(me_r + i, NR)
-            remote_r(psnd.at[it, q], gath.at[it, q, me_r], gath_send.at[it], gath_recv.at[it, q], to).start()
-            return 0
-
-        lax.fori_loop(1, NR, one, 0)
+        dst = gath.at[it, q, me_r]
+        for i in range(1, NX):
+            remote_r(psnd.at[it, q], dst, gath_send.at[it], gath_recv.at[it, q, 0], along_x(i) * 2 + me_y).start()
+        remote_r(psnd.at[it, q], dst, gath_send.at[it], gath_recv.at[it, q, 1], beside).start()
+
+    def pass_plus(it, q):
+        await_bytes(gath.at[it, q, 0], gath_recv.at[it, q, 1])
+        block = gath.at[it, q, beside, pl.ds(0, HALF)]
+        for i in range(1, NX):
+            remote_r(block, block, gath_send.at[it], gath_recv.at[it, q, 2], along_x(i) * 2 + me_y).start()
+        await_bytes(gath.at[it, q, pl.ds(0, NX - 1)], gath_recv.at[it, q, 0])
+        for i in range(1, NX):
+            block = gath.at[it, q, along_x(i) * 2 + me_y, pl.ds(HALF, HALF)]
+            remote_r(block, block, gath_send.at[it], gath_recv.at[it, q, 3], beside).start()
 
     def fill_perm(i, _):
         perm[pl.ds(pl.multiple_of(i * 128, 128), 128), :] = reorder_rows(i * 128, 128, SL)
@@ -206,10 +221,13 @@
         return slice(c * FB * ML + g * GF * ML, c * FB * ML + (g + 1) * GF * ML)
 
     def forward(it, q):
-        await_bytes(gath.at[it, q, pl.ds(0, NR - 1)], gath_recv.at[it, q])
         dims = (((1,), (1,)), ((), ()))
         blocks = ([], [])
         for g in range(NG):
+            if g == 0:
+                await_bytes(gath.at[it, q, pl.ds(0, NX - 1), pl.ds(0, HALF)], gath_recv.at[it, q, 2])
+            if g == NG // 2:
+                await_bytes(gath.at[it, q, pl.ds(0, NX - 1), pl.ds(0, HALF)], gath_recv.at[it, q, 3])
             rows = slice(g * ROWS, (g + 1) * ROWS)
             values = jnp.concatenate([gath[it, q, r, rows, :] for r in range(NR)], axis=1)
             a = lax.dot_general(values, refl[refl_rows(0, g), :], dims, preferred_element_type=F32)
@@ -291,24 +309,49 @@
                 out = jnp.dot(left, refl[refl_rows(0, g), cols], preferred_element_type=F32)
                 out += jnp.dot(right, refl[refl_rows(1, g), cols], preferred_element_type=F32)
                 out = out.astype(BF16)
-                psum_snd[it, q, 2 * n, g * ROWS : (g + 1) * ROWS, :] = out[:, :128]
-                psum_snd[it, q, 2 * n + 1, g * ROWS : (g + 1) * ROWS, :] = out[:, 128:]
-        psum_rcv[it, q, me_r] = psum_snd[it, q, me_r]
-
-        def one(i, _):
-            to = lax.rem(me_r + i, NR)
+                rows = slice(g % 2 * ROWS, (g % 2 + 1) * ROWS)
+                for y in range(2):
+                    values = out[:, y * SL : (y + 1) * SL]
+                    if g < NG // 2:
+                        part_a[it, q, n, y, rows, :] = values
+                    else:
+                        part_b[it, q, y, n, rows, :] = values
+            if g == NG // 2 - 1:
+                for i in range(1, NX):
+                    remote_r(
+                        part_a.at[it, q, along_x(i)], from_x.at[it, q, NX - 1 - i], rs_send.at[it],
+                        rs_recv.at[it, q, 0], along_x(i) * 2 + me_y,
+                    ).start()
+        remote_r(
+            part_b.at[it, q, 1 - me_y], from_y.at[it, q], rs_send.at[it], rs_recv.at[it, q, 1], beside
+        ).start()
+
+    def pass_sums(it, q):
+        await_bytes(from_x.at[it, q], rs_recv.at[it, q, 0])
+        total = part_a[it, q, me_x, 1 - me_y].astype(F32)
+        for i in range(NX - 1):
+            total += from_x[it, q, i, 1 - me_y].astype(F32)
+        sum_a[it, q] = total.astype(BF16)
+        remote_r(sum_a.at[it, q], rest_a.at[it, q], rs_send.at[it], rs_recv.at[it, q, 2], beside).start()
+        await_bytes(from_y.at[it, q], rs_recv.at[it, q, 1])
+        for i in range(1, NX):
+            x = along_x(i)
+            total = part_b[it, q, me_y, x].astype(F32) + from_y[it, q, x].astype(F32)
+            sum_b[it, q, i - 1] = total.astype(BF16)
             remote_r(
-                psum_snd.at[it, q, to], psum_rcv.at[it, q, me_r], rs_send.at[it], rs_recv.at[it, q], to
+                sum_b.at[it, q, i - 1], rest_b.at[it, q, NX - 1 - i], rs_send.at[it], rs_recv.at[it, q, 3],
+                x * 2 + me_y,
             ).start()
-            return 0
-
-        lax.fori_loop(1, NR, one, 0)
 
     def add_up(it, q):
-        await_bytes(psum_rcv.at[it, q, pl.ds(0, NR - 1)], rs_recv.at[it, q])
-        total = psum_rcv[it, q, 0].astype(F32)
-        for r in range(1, NR):
-            total += psum_rcv[it, q, r].astype(F32)
+        await_bytes(rest_a.at[it, q], rs_recv.at[it, q, 2])
+        await_bytes(rest_b.at[it, q], rs_recv.at[it, q, 3])
+        first = part_a[it, q, me_x, me_y].astype(F32) + rest_a[it, q].astype(F32)
+        second = part_b[it, q, me_y, me_x].astype(F32) + from_y[it, q, me_x].astype(F32)
+        for i in range(NX - 1):
+            first += from_x[it, q, i, me_y].astype(F32)
+            second += rest_b[it, q, i].astype(F32)
+        total = jnp.concatenate([first, second], axis=0)
         for c in range(2):
             for i in range(4):
                 to = PLUS_AT[c][4 * q + i]
@@ -378,23 +421,29 @@
             out_minus[...] = lax.dot_general(minus, perm_m[...], dims, preferred_element_type=F32)
 
     def iteration(it, _):
+        pass_plus(it, 0)
+        pass_plus(it, 1)
+        pass_plus(it, 2)
         forward(it, 0)
+        forward(it, 1)
+        forward(it, 2)
         window_minus(it, 0)
-        forward(it, 1)
         window_minus(it, 1)
-        forward(it, 2)
+        window_minus(it, 2)
         adjoint(it, 0)
-        window_minus(it, 2)
         adjoint(it, 1)
         adjoint(it, 2)
+        pass_sums(it, 0)
+        pass_sums(it, 1)
+        pass_sums(it, 2)
         add_up(it, 0)
+        add_up(it, 1)
+        add_up(it, 2)
+        window_plus(it, 0)
         finish_minus(it)
-        add_up(it, 1)
-        window_plus(it, 0)
-        add_up(it, 2)
         window_plus(it, 1)
+        window_plus(it, 2)
         update(it, 0)
-        window_plus(it, 2)
         update(it, 1)
         update(it, 2)
         return 0
@@ -460,18 +509,24 @@
             pltpu.VMEM((ITERS, NK, 128), BF16),
             pltpu.VMEM((ITERS, NQ, 2, FB, 128), BF16),
             pltpu.VMEM((2 * FB, 1024), F32),
-            pltpu.VMEM((ITERS, NQ, NR, NG * ROWS, SL), BF16),
-            pltpu.VMEM((ITERS, NQ, NR, NG * ROWS, SL), BF16),
+            pltpu.VMEM((ITERS, NQ, NX, 2, HALF, SL), BF16),
+            pltpu.VMEM((ITERS, NQ, 2, NX, HALF, SL), BF16),
+            pltpu.VMEM((ITERS, NQ, NX - 1, 2, HALF, SL), BF16),
+            pltpu.VMEM((ITERS, NQ, NX, HALF, SL), BF16),
+            pltpu.VMEM((ITERS, NQ, HALF, SL), BF16),
+            pltpu.VMEM((ITERS, NQ, NX - 1, HALF, SL), BF16),
+            pltpu.VMEM((ITERS, NQ, HALF, SL), BF16),
+            pltpu.VMEM((ITERS, NQ, NX - 1, HALF, SL), BF16),
             pltpu.VMEM((ITERS, NQ, 8, FB, SL), BF16),
             pltpu.VMEM((ITERS, NK, SL), BF16),
             pltpu.VMEM((ITERS, NK, SL), BF16),
             pltpu.VMEM((ITERS, NQ, 8, FB, SL), BF16),
             pltpu.VMEM((256, TW), BF16),
             dma((2,)),
-            dma((ITERS,)), dma((ITERS, NQ)),
+            dma((ITERS,)), dma((ITERS, NQ, 4)),
             dma((ITERS,)), dma((ITERS,)),
             dma((ITERS,)), dma((ITERS, NQ)),
-            dma((ITERS,)), dma((ITERS, NQ)),
+            dma((ITERS,)), dma((ITERS, NQ, 4)),
             dma((ITERS,)), dma((ITERS,)),
             dma((ITERS,)), dma((ITERS, NQ)),
         ],

time: 147 us -> 128 us (0.87)
  Pallas kernels: 143 us -> 123 us
    pallas_call x1, Pallas kernels: 143 us -> 123 us  [local(): pl.pallas_call(kernel, out_shape=(jax.ShapeDtypeStruct((2 * FB, ML * PS),...]
where the time goes in v3:
time: 128 us; the launch traced here: 127 us
  Pallas kernels  123 us (96%)
  local copies, waits for them, and re-layouts  3.31 us (3%)
    pallas_call x1, Pallas kernels, local(): pl.pallas_call(kernel, out_shape=(jax.ShapeDtypeStruct((2 * FB, ML * PS),...  123 us
    unnamed x2, local copies, waits for them, and re-layouts  3.31 us

profile of v3, /device:TPU:1, one launch (start us, length us, event | category | flops | bytes accessed | tf_op | source)
XLA Modules:
  0.0 126.8 jit_solution(13396907624786978884)
XLA Ops:
  0.6 122.9 %shard_map.68 = (f32[64,384]{1,0:T(8,128)}, f32[64,1536]{1,0:T(8,128)}) custom-call(bf16[2048,1024]{1,0:T(8,128)(2,1)} %bitcast.6, f32[2,1024,1024]{2,1,0:T(8,128)} %constant.2.clone.tab_hbm, f32[64,1536]{1,0:T(8,128)} %bitcast.7, s32[12,32]{1,0:T(8,128)} %bitcast.10, s32[12,128]{1,0:T(8,128)} %bitcast.11), custom_call_target="tpu_custom_call" | custom-call | tf_op jit(solution)/shard_map/pallas_call | solution.py:489
  123.5 1.5 %copy.9 = f32[2,32,384]{2,1,0:T(8,128)} copy(f32[2,32,384]{2,1,0:T(8,128)} %bitcast.9) | data formatting | bytes 196608
  125.0 1.8 %copy.10 = f32[2,32,1536]{2,1,0:T(8,128)} copy(f32[2,32,1536]{2,1,0:T(8,128)} %bitcast.8) | data formatting | bytes 786432

commit v4 on v2

--- a/solution.py
+++ b/solution.py
@@ -14,9 +14,11 @@
 FB = 32
 NB = 32
 NR = 8
+NX = 4
 GF = 8
 NG = FB // GF
 ROWS = 2 * 4 * GF
+HALF = NG * ROWS // 2
 ML = 32
 SL = 128
 NK = FB * NB
@@ -58,19 +60,27 @@
 
 
 def kernel(
-    refl_hbm, tab_hbm, plus_ref, onm_ref, onp_ref,
+    refl_hbm, tab_hbm, plus_hbm, onm_ref, onp_ref,
     out_minus, out_plus,
-    refl, tab_full, tab, perm, perm_m, spread, pinit, psnd, gath, msnd, xm, ymsnd, ym, wide, psum_snd, psum_rcv,
-    xsnd, xp, ypsnd, wp, eo,
+    plus_ref, refl, refl_t, tab_full, tab, perm, perm_m, spread, pinit, psnd, gath, msnd, xm, ymsnd, ym, wide,
+    partial, from_far, from_x, from_y, sums, rests, xsnd, xp, ypsnd, wp, eo,
     load_sem, gath_send, gath_recv, xm_send, xm_recv, ym_send, ym_recv, rs_send, rs_recv, xp_send, xp_recv,
     wp_send, wp_recv,
 ):
     me_f = lax.axis_index("freq")
     me_r = lax.axis_index("rcv")
     part = me_f // (NB // 2)
+    me_x, me_y = me_r // 2, lax.rem(me_r, 2)
+    beside = me_x * 2 + (1 - me_y)
+
+    def along_x(i):
+        return lax.rem(me_x + i, NX)
+
 
     load_refl = pltpu.make_async_copy(refl_hbm, refl, load_sem.at[0])
     load_tab = pltpu.make_async_copy(tab_hbm.at[part], tab_full, load_sem.at[1])
+    load_plus = pltpu.make_async_copy(plus_hbm, plus_ref, load_sem.at[2])
+    load_plus.start()
     load_refl.start()
     load_tab.start()
 
@@ -122,21 +132,37 @@
     def plus_places(q):
         return [PLUS_AT[c][4 * q + i] for c in range(2) for i in range(4)]
 
+    def row_x(i):
+        return along_x(i) * 2 + me_y
+
     def send_plus(it, q):
         gath[it, q, me_r] = psnd[it, q]
-
-        def one(i, _):
-            to = lax.rem(me_r + i, NR)
-            remote_r(psnd.at[it, q], gath.at[it, q, me_r], gath_send.at[it], gath_recv.at[it, q], to).start()
-            return 0
-
-        lax.fori_loop(1, NR, one, 0)
+        dst = gath.at[it, q, me_r]
+        for i in (1, 3):
+            remote_r(psnd.at[it, q], dst, gath_send.at[it], gath_recv.at[it, q, 0], row_x(i)).start()
+        remote_r(psnd.at[it, q], dst, gath_send.at[it], gath_recv.at[it, q, 1], beside).start()
+
+    def pass_plus(it, q):
+        def pass_on(r, start, rows, sem, to):
+            block = gath.at[it, q, r, pl.ds(start, rows)]
+            remote_r(block, block, gath_send.at[it], gath_recv.at[it, q, sem], to).start()
+
+        await_bytes(gath.at[it, q, 0], gath_recv.at[it, q, 1])
+        pass_on(beside, 0, 4 * ROWS, 2, row_x(2))
+        pass_on(beside, 0, ROWS, 4, row_x(1))
+        pass_on(beside, 0, ROWS, 3, row_x(3))
+        await_bytes(gath.at[it, q, pl.ds(0, 2)], gath_recv.at[it, q, 0])
+        pass_on(row_x(1), ROWS, 3 * ROWS, 5, beside)
+        pass_on(row_x(3), ROWS, 3 * ROWS, 5, beside)
+        pass_on(row_x(3), 0, HALF, 4, row_x(1))
+        pass_on(row_x(1), HALF, HALF, 3, row_x(3))
 
     def fill_perm(i, _):
         perm[pl.ds(pl.multiple_of(i * 128, 128), 128), :] = reorder_rows(i * 128, 128, SL)
         return 0
 
     lax.fori_loop(0, PS, fill_perm, 0)
+    load_plus.wait()
     high = plus_ref[...].astype(BF16)
     left = plus_ref[...] - high.astype(F32)
     middle = left.astype(BF16)
@@ -174,6 +200,10 @@
 
     lax.fori_loop(0, NK // 128, split_tab, 0)
     load_refl.wait()
+    for g in range(NG):
+        for c in range(2):
+            block = refl[c * FB * ML + g * GF * ML : c * FB * ML + (g + 1) * GF * ML, :]
+            refl_t[g, :, c * GF * ML : (c + 1) * GF * ML] = jnp.transpose(block)
 
     def window(x, onsets, y, send_chunk):
         until = jnp.transpose(jnp.broadcast_to(onsets, (128, 128)))
@@ -206,14 +236,18 @@
         return slice(c * FB * ML + g * GF * ML, c * FB * ML + (g + 1) * GF * ML)
 
     def forward(it, q):
-        await_bytes(gath.at[it, q, pl.ds(0, NR - 1)], gath_recv.at[it, q])
-        dims = (((1,), (1,)), ((), ()))
         blocks = ([], [])
         for g in range(NG):
+            if g == 0:
+                await_bytes(gath.at[it, q, 0, pl.ds(0, 3 * ROWS)], gath_recv.at[it, q, 3])
+                await_bytes(gath.at[it, q, 0, pl.ds(0, 3 * ROWS)], gath_recv.at[it, q, 4])
+                await_bytes(gath.at[it, q, 0], gath_recv.at[it, q, 2])
+            if g == 1:
+                await_bytes(gath.at[it, q, pl.ds(0, 2), pl.ds(0, 3 * ROWS)], gath_recv.at[it, q, 5])
             rows = slice(g * ROWS, (g + 1) * ROWS)
             values = jnp.concatenate([gath[it, q, r, rows, :] for r in range(NR)], axis=1)
-            a = lax.dot_general(values, refl[refl_rows(0, g), :], dims, preferred_element_type=F32)
-            b = lax.dot_general(values, refl[refl_rows(1, g), :], dims, preferred_element_type=F32)
+            both = jnp.dot(values, refl_t[g], preferred_element_type=F32)
+            a, b = both[:, : GF * ML], both[:, GF * ML :]
             parts = (a[:half] - b[half:], b[:half] + a[half:])
             for c in range(2):
                 own = jnp.where(same, parts[c], 0.0)
@@ -291,24 +325,51 @@
                 out = jnp.dot(left, refl[refl_rows(0, g), cols], preferred_element_type=F32)
                 out += jnp.dot(right, refl[refl_rows(1, g), cols], preferred_element_type=F32)
                 out = out.astype(BF16)
-                psum_snd[it, q, 2 * n, g * ROWS : (g + 1) * ROWS, :] = out[:, :128]
-                psum_snd[it, q, 2 * n + 1, g * ROWS : (g + 1) * ROWS, :] = out[:, 128:]
-        psum_rcv[it, q, me_r] = psum_snd[it, q, me_r]
-
-        def one(i, _):
-            to = lax.rem(me_r + i, NR)
+                for y in range(2):
+                    partial[it, q, n, y, g * ROWS : (g + 1) * ROWS, :] = out[:, y * SL : (y + 1) * SL]
+
+        def send(x, y, start, rows, dst, sem, to):
+            src = partial.at[it, q, x, y, pl.ds(start, rows)]
+            remote_r(src, dst, rs_send.at[it], rs_recv.at[it, q, sem], to).start()
+
+        send(along_x(2), 1 - me_y, 0, 4 * ROWS, from_far.at[it, q], 0, row_x(2))
+        for k, i in enumerate((1, 3)):
+            send(along_x(i), 1 - me_y, ROWS, 3 * ROWS, from_y.at[it, q, k], 3, beside)
+        for k, i in enumerate((1, 3)):
+            there = from_x.at[it, q, 1 - k]
+            send(along_x(2), me_y, k * HALF, HALF, there.at[pl.ds(0, HALF)], 2 - k, row_x(i))
+            send(along_x(i), 1 - me_y, 0, ROWS, there.at[pl.ds(HALF, ROWS)], 2 - k, row_x(i))
+
+    def pass_sums(it, q):
+        def pass_on(total, slot, sem, to):
+            sums[it, q, slot] = total.astype(BF16)
             remote_r(
-                psum_snd.at[it, q, to], psum_rcv.at[it, q, me_r], rs_send.at[it], rs_recv.at[it, q], to
+                sums.at[it, q, slot], rests.at[it, q, sem - 4], rs_send.at[it], rs_recv.at[it, q, sem], to
             ).start()
-            return 0
-
-        lax.fori_loop(1, NR, one, 0)
+
+        await_bytes(from_x.at[it, q, 0], rs_recv.at[it, q, 1])
+        await_bytes(from_x.at[it, q, 1], rs_recv.at[it, q, 2])
+        await_bytes(from_far.at[it, q], rs_recv.at[it, q, 0])
+        total = partial[it, q, me_x, 1 - me_y].astype(F32) + from_far[it, q].astype(F32)
+        quarter = from_x[it, q, 0, HALF:, :].astype(F32) + from_x[it, q, 1, HALF:, :].astype(F32)
+        pass_on(jnp.concatenate([total[:ROWS] + quarter, total[ROWS:]], axis=0), 2, 6, beside)
+        await_bytes(from_y.at[it, q], rs_recv.at[it, q, 3])
+        for k, i in enumerate((1, 3)):
+            total = partial[it, q, along_x(i), me_y].astype(F32)
+            more = from_y[it, q, k].astype(F32)
+            half = from_x[it, q, 1 - k, :HALF, :].astype(F32)
+            if k == 0:
+                pieces = [total[:ROWS] + half[:ROWS], total[ROWS:HALF] + half[ROWS:] + more[:ROWS]]
+                pieces.append(total[HALF:] + more[ROWS:])
+            else:
+                pieces = [total[:ROWS], total[ROWS:HALF] + more[:ROWS], total[HALF:] + half + more[ROWS:]]
+            pass_on(jnp.concatenate(pieces, axis=0), k, 5 - k, row_x(i))
 
     def add_up(it, q):
-        await_bytes(psum_rcv.at[it, q, pl.ds(0, NR - 1)], rs_recv.at[it, q])
-        total = psum_rcv[it, q, 0].astype(F32)
-        for r in range(1, NR):
-            total += psum_rcv[it, q, r].astype(F32)
+        total = partial[it, q, me_x, me_y].astype(F32)
+        for k in range(3):
+            await_bytes(rests.at[it, q, k], rs_recv.at[it, q, 4 + k])
+            total += rests[it, q, k].astype(F32)
         for c in range(2):
             for i in range(4):
                 to = PLUS_AT[c][4 * q + i]
@@ -378,23 +439,29 @@
             out_minus[...] = lax.dot_general(minus, perm_m[...], dims, preferred_element_type=F32)
 
     def iteration(it, _):
+        pass_plus(it, 0)
+        pass_plus(it, 1)
         forward(it, 0)
+        pass_plus(it, 2)
+        forward(it, 1)
+        forward(it, 2)
         window_minus(it, 0)
-        forward(it, 1)
         window_minus(it, 1)
-        forward(it, 2)
+        window_minus(it, 2)
         adjoint(it, 0)
-        window_minus(it, 2)
         adjoint(it, 1)
+        pass_sums(it, 0)
         adjoint(it, 2)
+        pass_sums(it, 1)
+        pass_sums(it, 2)
         add_up(it, 0)
+        add_up(it, 1)
+        add_up(it, 2)
+        window_plus(it, 0)
         finish_minus(it)
-        add_up(it, 1)
-        window_plus(it, 0)
-        add_up(it, 2)
         window_plus(it, 1)
+        window_plus(it, 2)
         update(it, 0)
-        window_plus(it, 2)
         update(it, 1)
         update(it, 2)
         return 0
@@ -443,10 +510,12 @@
             jax.ShapeDtypeStruct((2 * FB, ML * PS), F32),
             jax.ShapeDtypeStruct((2 * FB, SL * PS), F32),
         ),
-        in_specs=[hbm, hbm, vmem, vmem, vmem],
+        in_specs=[hbm, hbm, hbm, vmem, vmem],
         out_specs=(vmem, vmem),
         scratch_shapes=[
+            pltpu.VMEM((2 * FB, SL * PS), F32),
             pltpu.VMEM((2 * FB * ML, 1024), BF16),
+            pltpu.VMEM((NG, 1024, 2 * GF * ML), BF16),
             pltpu.VMEM((NK, NK), F32),
             pltpu.VMEM((2, NK, NK), BF16),
             pltpu.VMEM((SL * PS, SL * PS), BF16),
@@ -460,18 +529,22 @@
             pltpu.VMEM((ITERS, NK, 128), BF16),
             pltpu.VMEM((ITERS, NQ, 2, FB, 128), BF16),
             pltpu.VMEM((2 * FB, 1024), F32),
-            pltpu.VMEM((ITERS, NQ, NR, NG * ROWS, SL), BF16),
-            pltpu.VMEM((ITERS, NQ, NR, NG * ROWS, SL), BF16),
+            pltpu.VMEM((ITERS, NQ, NX, 2, 4 * ROWS, SL), BF16),
+            pltpu.VMEM((ITERS, NQ, 4 * ROWS, SL), BF16),
+            pltpu.VMEM((ITERS, NQ, 2, 3 * ROWS, SL), BF16),
+            pltpu.VMEM((ITERS, NQ, 2, 3 * ROWS, SL), BF16),
+            pltpu.VMEM((ITERS, NQ, 3, 4 * ROWS, SL), BF16),
+            pltpu.VMEM((ITERS, NQ, 3, 4 * ROWS, SL), BF16),
             pltpu.VMEM((ITERS, NQ, 8, FB, SL), BF16),
             pltpu.VMEM((ITERS, NK, SL), BF16),
             pltpu.VMEM((ITERS, NK, SL), BF16),
             pltpu.VMEM((ITERS, NQ, 8, FB, SL), BF16),
             pltpu.VMEM((256, TW), BF16),
-            dma((2,)),
-            dma((ITERS,)), dma((ITERS, NQ)),
+            dma((3,)),
+            dma((ITERS,)), dma((ITERS, NQ, 6)),
             dma((ITERS,)), dma((ITERS,)),
             dma((ITERS,)), dma((ITERS, NQ)),
-            dma((ITERS,)), dma((ITERS, NQ)),
+            dma((ITERS,)), dma((ITERS, NQ, 7)),
             dma((ITERS,)), dma((ITERS,)),
             dma((ITERS,)), dma((ITERS, NQ)),
         ],

time: 147 us -> 122 us (0.83)
  Pallas kernels: 143 us -> 117 us
    pallas_call x1, Pallas kernels: 143 us -> 117 us  [local(): pl.pallas_call(kernel, out_shape=(jax.ShapeDtypeStruct((2 * FB, ML * PS),...]
where the time goes in v4:
time: 122 us; the launch traced here: 121 us
  Pallas kernels  117 us (96%)
  local copies, waits for them, and re-layouts  3.31 us (3%)
    pallas_call x1, Pallas kernels, local(): pl.pallas_call(kernel, out_shape=(jax.ShapeDtypeStruct((2 * FB, ML * PS),...  117 us
    unnamed x2, local copies, waits for them, and re-layouts  3.31 us

profile of v4, /device:TPU:1, one launch (start us, length us, event | category | flops | bytes accessed | tf_op | source)
XLA Modules:
  0.0 121.0 jit_solution(1244034419755667190)
XLA Ops:
  0.6 117.1 %shard_map.68 = (f32[64,384]{1,0:T(8,128)}, f32[64,1536]{1,0:T(8,128)}) custom-call(bf16[2048,1024]{1,0:T(8,128)(2,1)} %bitcast.6, f32[2,1024,1024]{2,1,0:T(8,128)} %constant.2.clone.tab_hbm, f32[64,1536]{1,0:T(8,128)} %bitcast.7, s32[12,32]{1,0:T(8,128)} %bitcast.10, s32[12,128]{1,0:T(8,128)} %bitcast.11), custom_call_target="tpu_custom_call" | custom-call | tf_op jit(solution)/shard_map/pallas_call | solution.py:507
  117.7 1.5 %copy.9 = f32[2,32,384]{2,1,0:T(8,128)} copy(f32[2,32,384]{2,1,0:T(8,128)} %bitcast.9) | data formatting | bytes 196608
  119.3 1.8 %copy.10 = f32[2,32,1536]{2,1,0:T(8,128)} copy(f32[2,32,1536]{2,1,0:T(8,128)} %bitcast.8) | data formatting | bytes 786432

commit v5 on v4

--- a/solution.py
+++ b/solution.py
@@ -52,7 +52,7 @@
     return jnp.where(hit, 1.0, 0.0).astype(BF16)
 
 
-MINUS_AT = ((3, 11, 5), (25, 17, 31))
+MINUS_AT = (((3, 11), (5, 13), (2, 10)), ((19, 27), (21, 29), (18, 26)))
 PLUS_AT = (
     (0, 4, 8, 12, 2, 6, 10, 14, 1, 7, 9, 15),
     (18, 22, 26, 30, 16, 20, 24, 28, 19, 21, 27, 29),
@@ -70,6 +70,7 @@
     me_f = lax.axis_index("freq")
     me_r = lax.axis_index("rcv")
     part = me_f // (NB // 2)
+    z_half = lax.rem(me_f, NB // 2) // 8
     me_x, me_y = me_r // 2, lax.rem(me_r, 2)
     beside = me_x * 2 + (1 - me_y)
 
@@ -127,7 +128,7 @@
         return found
 
     def minus_places(q):
-        return [MINUS_AT[c][q] for c in range(2)]
+        return [place for c in range(2) for place in MINUS_AT[c][q]]
 
     def plus_places(q):
         return [PLUS_AT[c][4 * q + i] for c in range(2) for i in range(4)]
@@ -205,7 +206,7 @@
             block = refl[c * FB * ML + g * GF * ML : c * FB * ML + (g + 1) * GF * ML, :]
             refl_t[g, :, c * GF * ML : (c + 1) * GF * ML] = jnp.transpose(block)
 
-    def window(x, onsets, y, send_chunk):
+    def window(x, onsets, y, send_chunk, chunks):
         until = jnp.transpose(jnp.broadcast_to(onsets, (128, 128)))
         until = jnp.concatenate([until, until], axis=1)
         traces = jnp.transpose(x[...])
@@ -219,8 +220,8 @@
             top = in_time.astype(BF16)
             eo[:128, cols] = top
             eo[128:, cols] = (in_time - top.astype(F32)).astype(BF16)
-        for n in range(NK // 256):
-            cols = slice(n * 256, (n + 1) * 256)
+        for n in chunks:
+            cols = pl.ds(pl.multiple_of(n * 256, 256), 256)
             both = jnp.dot(eo[...], tab[0, :TW, cols], preferred_element_type=F32)
             small = jnp.dot(eo[:128, :], tab[1, :TW, cols], preferred_element_type=F32)
             y[cols, :] = jnp.transpose(both[:128] + (both[128:] + small)).astype(BF16)
@@ -259,16 +260,16 @@
                     block = jnp.where(quad_lane == i, own[i * GF : (i + 1) * GF], block)
                 blocks[c].append(block)
         for c in range(2):
-            to = MINUS_AT[c][q]
             msnd[it, q, c] = (jnp.concatenate(blocks[c], axis=0) * k_scale).astype(BF16)
-
-            @pl.when(me_f == to)
-            def _():
-                xm[it, my_rows, :] = msnd[it, q, c]
-
-            @pl.when(me_f != to)
-            def _():
-                remote_f(msnd.at[it, q, c], xm.at[it, my_rows], xm_send.at[it], xm_recv.at[it], to).start()
+            for to in MINUS_AT[c][q]:
+
+                @pl.when(me_f == to)
+                def _():
+                    xm[it, my_rows, :] = msnd[it, q, c]
+
+                @pl.when(me_f != to)
+                def _():
+                    remote_f(msnd.at[it, q, c], xm.at[it, my_rows], xm_send.at[it], xm_recv.at[it], to).start()
 
     def scatter(it, buffer, dst, send, recv):
         def send_chunk(begin, count):
@@ -296,7 +297,7 @@
             await_bytes(xm.at[it, pl.ds(0, NK - FB)], xm_recv.at[it])
             onsets = jnp.concatenate([onm_ref[4 * q + i : 4 * q + i + 1, :] for i in range(4)], axis=1)
             send_chunk = scatter(it, ymsnd, ym.at[it, q, part], ym_send.at[it], ym_recv.at[it, q])
-            window(xm.at[it], onsets, ymsnd.at[it], send_chunk)
+            window(xm.at[it], onsets, ymsnd.at[it], send_chunk, (z_half, z_half + 2))
 
     def adjoint(it, q):
         here = any_of(minus_places(q))
@@ -396,7 +397,7 @@
                 point = jnp.where(any_of([PLUS_AT[c][4 * q + i] for c in range(2)]), i, point)
             onsets = onp_ref[pl.ds(4 * q + point, 1), :]
             send_chunk = scatter(it, ypsnd, wp.at[it, q, part * 4 + point], wp_send.at[it], wp_recv.at[it, q])
-            window(xp.at[it], onsets, ypsnd.at[it], send_chunk)
+            window(xp.at[it], onsets, ypsnd.at[it], send_chunk, range(NK // 256))
 
     def update(it, q):
         here = any_of(plus_places(q))
@@ -426,8 +427,10 @@
             change = lax.dot_general(
                 change, perm[:, q * 4 * SL : (q + 1) * 4 * SL], dims, preferred_element_type=F32
             )
-            before = plus_ref if q == 0 else out_plus
-            out_plus[...] = before[...] + change
+            if q < NQ - 1:
+                plus_ref[...] = change if q == 0 else plus_ref[...] + change
+            else:
+                out_plus[...] = (plus_ref[...] + change).astype(BF16)
 
     def finish_minus(it):
         @pl.when(it == ITERS - 1)
@@ -436,13 +439,14 @@
                 [jnp.concatenate([ym[it, q, c] for q in range(NQ)], axis=1) for c in range(2)], axis=0
             )
             dims = (((1,), (1,)), ((), ()))
-            out_minus[...] = lax.dot_general(minus, perm_m[...], dims, preferred_element_type=F32)
+            minus = lax.dot_general(minus, perm_m[...], dims, preferred_element_type=F32)
+            out_minus[...] = minus.astype(BF16)
 
     def iteration(it, _):
         pass_plus(it, 0)
         pass_plus(it, 1)
+        pass_plus(it, 2)
         forward(it, 0)
-        pass_plus(it, 2)
         forward(it, 1)
         forward(it, 2)
         window_minus(it, 0)
@@ -450,8 +454,8 @@
         window_minus(it, 2)
         adjoint(it, 0)
         adjoint(it, 1)
+        adjoint(it, 2)
         pass_sums(it, 0)
-        adjoint(it, 2)
         pass_sums(it, 1)
         pass_sums(it, 2)
         add_up(it, 0)
@@ -477,12 +481,12 @@
 
         @pl.when(is_minus)
         def _():
-            await_bytes(xm.at[it, pl.ds(0, (WM - 1) * FB)], xm_send.at[it])
-            await_bytes(ymsnd.at[it, pl.ds(0, NK - FB)], ym_send.at[it])
+            await_bytes(xm.at[it, pl.ds(0, (2 * WM - 1) * FB)], xm_send.at[it])
+            await_bytes(ymsnd.at[it, pl.ds(0, NK // 2 - FB)], ym_send.at[it])
 
         @pl.when(jnp.logical_not(is_minus))
         def _():
-            await_bytes(msnd.at[it], xm_send.at[it])
+            await_bytes(xm.at[it, pl.ds(0, 2 * WM * FB)], xm_send.at[it])
 
         @pl.when(is_plus)
         def _():
@@ -496,6 +500,11 @@
         return 0
 
     lax.fori_loop(0, ITERS, drain, 0)
+
+
+def widen(minus_ref, change_ref, plus_ref, out_minus, out_plus):
+    out_minus[...] = minus_ref[...].astype(F32)
+    out_plus[...] = plus_ref[...] + change_ref[...].astype(F32)
 
 
 def local(reflection, plus_init, onset_receiver, onset_source):
@@ -504,11 +513,12 @@
     vmem = pl.BlockSpec(memory_space=pltpu.VMEM)
     hbm = pl.BlockSpec(memory_space=pl.ANY)
     dma = pltpu.SemaphoreType.DMA
-    out_minus, out_plus = pl.pallas_call(
+    plus_rows = plus_init.reshape(2 * FB, SL * PS)
+    minus, change = pl.pallas_call(
         kernel,
         out_shape=(
-            jax.ShapeDtypeStruct((2 * FB, ML * PS), F32),
-            jax.ShapeDtypeStruct((2 * FB, SL * PS), F32),
+            jax.ShapeDtypeStruct((2 * FB, ML * PS), BF16),
+            jax.ShapeDtypeStruct((2 * FB, SL * PS), BF16),
         ),
         in_specs=[hbm, hbm, hbm, vmem, vmem],
         out_specs=(vmem, vmem),
@@ -554,10 +564,19 @@
     )(
         reflection.reshape(2 * FB * ML, 1024),
         jnp.asarray(tables()),
-        plus_init.reshape(2 * FB, SL * PS),
+        plus_rows,
         onm,
         onp,
     )
+    out_minus, out_plus = pl.pallas_call(
+        widen,
+        out_shape=(
+            jax.ShapeDtypeStruct((2 * FB, ML * PS), F32),
+            jax.ShapeDtypeStruct((2 * FB, SL * PS), F32),
+        ),
+        in_specs=[vmem, vmem, vmem],
+        out_specs=(vmem, vmem),
+    )(minus, change, plus_rows)
     return out_minus.reshape(2, FB, ML * PS), out_plus.reshape(2, FB, SL * PS)
 
 

time: 122 us -> 117 us (0.959)
  local copies, waits for them, and re-layouts: 3.31 us -> 0 us
    unnamed x2 -> x0, local copies, waits for them, and re-layouts: 3.31 us -> none
    pallas_call x1, Pallas kernels: 117 us -> 114 us  [local(): pl.pallas_call(kernel, out_shape=(jax.ShapeDtypeStruct((2 * FB, ML * PS),...]
    pallas_call x0 -> x1, Pallas kernels: none -> 1.92 us  [local(): pl.pallas_call(widen, out_shape=(jax.ShapeDtypeStruct((2 * FB, ML * PS),...]
where the time goes in v5:
time: 117 us; the launch traced here: 116 us
  Pallas kernels  116 us (99%)
    pallas_call x1, Pallas kernels, local(): pl.pallas_call(kernel, out_shape=(jax.ShapeDtypeStruct((2 * FB, ML * PS),...  114 us

profile of v5, /device:TPU:1, one launch (start us, length us, event | category | flops | bytes accessed | tf_op | source)
XLA Modules:
  0.0 116.4 jit_solution(6070314332087228468)
XLA Ops:
  0.6 113.8 %shard_map.68 = (bf16[64,384]{1,0:T(8,128)(2,1)}, bf16[64,1536]{1,0:T(8,128)(2,1)}) custom-call(bf16[2048,1024]{1,0:T(8,128)(2,1)} %bitcast.6, f32[2,1024,1024]{2,1,0:T(8,128)} %constant.2.clone.tab_hbm, f32[64,1536]{1,0:T(8,128)} %bitcast.7, s32[12,32]{1,0:T(8,128)} %bitcast.9, s32[12,128]{1,0:T(8,128)} %bitcast.10), custom_call_target="tpu_custom_call" | custom-call | tf_op jit(solution)/shard_map/pallas_call | solution.py:517
  114.5 1.9 %shard_map.69 = (f32[64,384]{1,0:T(8,128)}, f32[64,1536]{1,0:T(8,128)}) custom-call(bf16[64,384]{1,0:T(8,128)(2,1)} %get-tuple-element.6.minus_ref, bf16[64,1536]{1,0:T(8,128)(2,1)} %get-tuple-element.7.change_ref, f32[64,1536]{1,0:T(8,128)} %bitcast.8), custom_call_target="tpu_custom_call" | custom-call | tf_op jit(solution)/shard_map/pallas_call | solution.py:571

commit v6 on v5

--- a/solution.py
+++ b/solution.py
@@ -45,6 +45,14 @@
     return jnp.where(lane == target, 1.0, 0.0).astype(BF16)
 
 
+def reorder_back_rows(start, rows, count):
+    index = start + lax.broadcasted_iota(jnp.int32, (rows, 1), 0)
+    point = index // count
+    target = (index - point * count) * PS + point
+    lane = lax.broadcasted_iota(jnp.int32, (rows, PS * count), 1)
+    return jnp.where(lane == target, 1.0, 0.0).astype(BF16)
+
+
 def spreading():
     row = lax.broadcasted_iota(jnp.int32, (4 * ML, 4 * GF * ML), 0)
     lane = lax.broadcasted_iota(jnp.int32, (4 * ML, 4 * GF * ML), 1)
@@ -62,7 +70,7 @@
 def kernel(
     refl_hbm, tab_hbm, plus_hbm, onm_ref, onp_ref,
     out_minus, out_plus,
-    plus_ref, refl, refl_t, tab_full, tab, perm, perm_m, spread, pinit, psnd, gath, msnd, xm, ymsnd, ym, wide,
+    plus_ref, refl, refl_t, tab_full, tab, perm, perm_back, perm_m, spread, pinit, psnd, gath, msnd, xm, ymsnd, ym, wide,
     partial, from_far, from_x, from_y, sums, rests, xsnd, xp, ypsnd, wp, eo,
     load_sem, gath_send, gath_recv, xm_send, xm_recv, ym_send, ym_recv, rs_send, rs_recv, xp_send, xp_recv,
     wp_send, wp_recv,
@@ -71,6 +79,7 @@
     me_r = lax.axis_index("rcv")
     part = me_f // (NB // 2)
     z_half = lax.rem(me_f, NB // 2) // 8
+    far_first = [2 * y + z for z in (1 - z_half, z_half) for y in (1 - part, part)]
     me_x, me_y = me_r // 2, lax.rem(me_r, 2)
     beside = me_x * 2 + (1 - me_y)
 
@@ -99,8 +108,9 @@
         )
         return 0
 
-    lax.fori_loop(1, NB, greet_f, 0)
     lax.fori_loop(1, NR, greet_r, 0)
+    lax.fori_loop(NB // 2 + 1, NB, greet_f, 0)
+    lax.fori_loop(1, NB // 2 + 1, greet_f, 0)
 
     row32 = lax.broadcasted_iota(jnp.int32, (FB, 128), 0)
     k_scale = jnp.where((row32 == 0) & (me_f == 0), 0.5, 1.0).astype(F32)
@@ -148,15 +158,15 @@
             block = gath.at[it, q, r, pl.ds(start, rows)]
             remote_r(block, block, gath_send.at[it], gath_recv.at[it, q, sem], to).start()
 
-        await_bytes(gath.at[it, q, 0], gath_recv.at[it, q, 1])
-        pass_on(beside, 0, 4 * ROWS, 2, row_x(2))
-        pass_on(beside, 0, ROWS, 4, row_x(1))
-        pass_on(beside, 0, ROWS, 3, row_x(3))
         await_bytes(gath.at[it, q, pl.ds(0, 2)], gath_recv.at[it, q, 0])
         pass_on(row_x(1), ROWS, 3 * ROWS, 5, beside)
         pass_on(row_x(3), ROWS, 3 * ROWS, 5, beside)
         pass_on(row_x(3), 0, HALF, 4, row_x(1))
         pass_on(row_x(1), HALF, HALF, 3, row_x(3))
+        await_bytes(gath.at[it, q, 0], gath_recv.at[it, q, 1])
+        pass_on(beside, 0, 4 * ROWS, 2, row_x(2))
+        pass_on(beside, 0, ROWS, 4, row_x(1))
+        pass_on(beside, 0, ROWS, 3, row_x(3))
 
     def fill_perm(i, _):
         perm[pl.ds(pl.multiple_of(i * 128, 128), 128), :] = reorder_rows(i * 128, 128, SL)
@@ -188,18 +198,21 @@
             pinit[p // 4, c * 4 + p % 4] = exact[c * FB : (c + 1) * FB, p * SL : (p + 1) * SL]
 
     spread[...] = spreading()
-    perm_m[...] = reorder_rows(0, ML * PS, ML)
+    perm_m[...] = reorder_back_rows(0, ML * PS, ML)
+
+    def fill_back(i, _):
+        perm_back[pl.ds(pl.multiple_of(i * 128, 128), 128), :] = reorder_back_rows(i * 128, 128, SL)
+        return 0
+
+    lax.fori_loop(0, PS, fill_back, 0)
     load_tab.wait()
 
-    def split_tab(i, _):
+    def round_tab(i, _):
         rows = pl.ds(pl.multiple_of(i * 128, 128), 128)
-        values = tab_full[rows, :]
-        top = values.astype(BF16)
-        tab[0, rows, :] = top
-        tab[1, rows, :] = (values - top.astype(F32)).astype(BF16)
+        tab[rows, :] = tab_full[rows, :].astype(BF16)
         return 0
 
-    lax.fori_loop(0, NK // 128, split_tab, 0)
+    lax.fori_loop(0, NK // 128, round_tab, 0)
     load_refl.wait()
     for g in range(NG):
         for c in range(2):
@@ -212,8 +225,7 @@
         traces = jnp.transpose(x[...])
         for n in range(TW // 256):
             cols = slice(n * 256, (n + 1) * 256)
-            in_time = jnp.dot(traces, tab[0, :, cols], preferred_element_type=F32)
-            in_time += jnp.dot(traces, tab[1, :, cols], preferred_element_type=F32)
+            in_time = jnp.dot(traces, tab[:, cols], preferred_element_type=F32)
             time = n * 256 + lax.broadcasted_iota(jnp.int32, (128, 256), 1)
             factor = jnp.where(time == 0, 1.0 / NK, 2.0 / NK).astype(F32)
             in_time = jnp.where(time < until, in_time * factor, 0.0)
@@ -222,9 +234,8 @@
             eo[128:, cols] = (in_time - top.astype(F32)).astype(BF16)
         for n in chunks:
             cols = pl.ds(pl.multiple_of(n * 256, 256), 256)
-            both = jnp.dot(eo[...], tab[0, :TW, cols], preferred_element_type=F32)
-            small = jnp.dot(eo[:128, :], tab[1, :TW, cols], preferred_element_type=F32)
-            y[cols, :] = jnp.transpose(both[:128] + (both[128:] + small)).astype(BF16)
+            both = jnp.dot(eo[...], tab[:TW, cols], preferred_element_type=F32)
+            y[cols, :] = jnp.transpose(both[:128] + both[128:]).astype(BF16)
             send_chunk(n * (256 // FB), 256 // FB)
 
     half = ROWS // 2
@@ -297,7 +308,7 @@
             await_bytes(xm.at[it, pl.ds(0, NK - FB)], xm_recv.at[it])
             onsets = jnp.concatenate([onm_ref[4 * q + i : 4 * q + i + 1, :] for i in range(4)], axis=1)
             send_chunk = scatter(it, ymsnd, ym.at[it, q, part], ym_send.at[it], ym_recv.at[it, q])
-            window(xm.at[it], onsets, ymsnd.at[it], send_chunk, (z_half, z_half + 2))
+            window(xm.at[it], onsets, ymsnd.at[it], send_chunk, far_first[2:])
 
     def adjoint(it, q):
         here = any_of(minus_places(q))
@@ -397,7 +408,7 @@
                 point = jnp.where(any_of([PLUS_AT[c][4 * q + i] for c in range(2)]), i, point)
             onsets = onp_ref[pl.ds(4 * q + point, 1), :]
             send_chunk = scatter(it, ypsnd, wp.at[it, q, part * 4 + point], wp_send.at[it], wp_recv.at[it, q])
-            window(xp.at[it], onsets, ypsnd.at[it], send_chunk, range(NK // 256))
+            window(xp.at[it], onsets, ypsnd.at[it], send_chunk, far_first)
 
     def update(it, q):
         here = any_of(plus_places(q))
@@ -423,9 +434,8 @@
             change = jnp.concatenate(
                 [jnp.concatenate([wp[it, q, c * 4 + i] for i in range(4)], axis=1) for c in range(2)], axis=0
             )
-            dims = (((1,), (1,)), ((), ()))
-            change = lax.dot_general(
-                change, perm[:, q * 4 * SL : (q + 1) * 4 * SL], dims, preferred_element_type=F32
+            change = jnp.dot(
+                change, perm_back[q * 4 * SL : (q + 1) * 4 * SL, :], preferred_element_type=F32
             )
             if q < NQ - 1:
                 plus_ref[...] = change if q == 0 else plus_ref[...] + change
@@ -438,8 +448,7 @@
             minus = jnp.concatenate(
                 [jnp.concatenate([ym[it, q, c] for q in range(NQ)], axis=1) for c in range(2)], axis=0
             )
-            dims = (((1,), (1,)), ((), ()))
-            minus = lax.dot_general(minus, perm_m[...], dims, preferred_element_type=F32)
+            minus = jnp.dot(minus, perm_m[...], preferred_element_type=F32)
             out_minus[...] = minus.astype(BF16)
 
     def iteration(it, _):
@@ -462,9 +471,9 @@
         add_up(it, 1)
         add_up(it, 2)
         window_plus(it, 0)
-        finish_minus(it)
         window_plus(it, 1)
         window_plus(it, 2)
+        finish_minus(it)
         update(it, 0)
         update(it, 1)
         update(it, 2)
@@ -527,7 +536,8 @@
             pltpu.VMEM((2 * FB * ML, 1024), BF16),
             pltpu.VMEM((NG, 1024, 2 * GF * ML), BF16),
             pltpu.VMEM((NK, NK), F32),
-            pltpu.VMEM((2, NK, NK), BF16),
+            pltpu.VMEM((NK, NK), BF16),
+            pltpu.VMEM((SL * PS, SL * PS), BF16),
             pltpu.VMEM((SL * PS, SL * PS), BF16),
             pltpu.VMEM((ML * PS, ML * PS), BF16),
             pltpu.VMEM((4 * ML, 4 * GF * ML), BF16),

time: 117 us -> 114 us (0.974)
  Pallas kernels: 116 us -> 114 us
    pallas_call x1, Pallas kernels: 114 us -> 112 us  [local(): pl.pallas_call(kernel, out_shape=(jax.ShapeDtypeStruct((2 * FB, ML * PS),...]
where the time goes in v6:
time: 114 us
  Pallas kernels  114 us (100%)
    pallas_call x1, Pallas kernels, local(): pl.pallas_call(kernel, out_shape=(jax.ShapeDtypeStruct((2 * FB, ML * PS),...  112 us

profile of v6, /device:TPU:1, one launch (start us, length us, event | category | flops | bytes accessed | tf_op | source)
XLA Modules:
  0.0 114.2 jit_solution(3304320786992347429)
XLA Ops:
  0.6 111.6 %shard_map.68 = (bf16[64,384]{1,0:T(8,128)(2,1)}, bf16[64,1536]{1,0:T(8,128)(2,1)}) custom-call(bf16[2048,1024]{1,0:T(8,128)(2,1)} %bitcast.6, f32[2,1024,1024]{2,1,0:T(8,128)} %constant.2.clone.tab_hbm, f32[64,1536]{1,0:T(8,128)} %bitcast.7, s32[12,32]{1,0:T(8,128)} %bitcast.9, s32[12,128]{1,0:T(8,128)} %bitcast.10), custom_call_target="tpu_custom_call" | custom-call | tf_op jit(solution)/shard_map/pallas_call | solution.py:526
  112.2 1.9 %shard_map.69 = (f32[64,384]{1,0:T(8,128)}, f32[64,1536]{1,0:T(8,128)}) custom-call(bf16[64,384]{1,0:T(8,128)(2,1)} %get-tuple-element.6.minus_ref, bf16[64,1536]{1,0:T(8,128)(2,1)} %get-tuple-element.7.change_ref, f32[64,1536]{1,0:T(8,128)} %bitcast.8), custom_call_target="tpu_custom_call" | custom-call | tf_op jit(solution)/shard_map/pallas_call | solution.py:581

commit v7 on v6

--- a/solution.py
+++ b/solution.py
@@ -219,9 +219,10 @@
             block = refl[c * FB * ML + g * GF * ML : c * FB * ML + (g + 1) * GF * ML, :]
             refl_t[g, :, c * GF * ML : (c + 1) * GF * ML] = jnp.transpose(block)
 
-    def window(x, onsets, y, send_chunk, chunks):
+    def window(x, onsets, y, send_chunk, chunks, arrival):
         until = jnp.transpose(jnp.broadcast_to(onsets, (128, 128)))
         until = jnp.concatenate([until, until], axis=1)
+        await_bytes(x.at[pl.ds(0, NK - FB)], arrival)
         traces = jnp.transpose(x[...])
         for n in range(TW // 256):
             cols = slice(n * 256, (n + 1) * 256)
@@ -305,10 +306,9 @@
     def window_minus(it, q):
         @pl.when(any_of(minus_places(q)))
         def _():
-            await_bytes(xm.at[it, pl.ds(0, NK - FB)], xm_recv.at[it])
             onsets = jnp.concatenate([onm_ref[4 * q + i : 4 * q + i + 1, :] for i in range(4)], axis=1)
             send_chunk = scatter(it, ymsnd, ym.at[it, q, part], ym_send.at[it], ym_recv.at[it, q])
-            window(xm.at[it], onsets, ymsnd.at[it], send_chunk, far_first[2:])
+            window(xm.at[it], onsets, ymsnd.at[it], send_chunk, far_first[2:], xm_recv.at[it])
 
     def adjoint(it, q):
         here = any_of(minus_places(q))
@@ -344,9 +344,9 @@
             src = partial.at[it, q, x, y, pl.ds(start, rows)]
             remote_r(src, dst, rs_send.at[it], rs_recv.at[it, q, sem], to).start()
 
-        send(along_x(2), 1 - me_y, 0, 4 * ROWS, from_far.at[it, q], 0, row_x(2))
         for k, i in enumerate((1, 3)):
             send(along_x(i), 1 - me_y, ROWS, 3 * ROWS, from_y.at[it, q, k], 3, beside)
+        send(along_x(2), 1 - me_y, 0, 4 * ROWS, from_far.at[it, q], 0, row_x(2))
         for k, i in enumerate((1, 3)):
             there = from_x.at[it, q, 1 - k]
             send(along_x(2), me_y, k * HALF, HALF, there.at[pl.ds(0, HALF)], 2 - k, row_x(i))
@@ -402,13 +402,12 @@
     def window_plus(it, q):
         @pl.when(any_of(plus_places(q)))
         def _():
-            await_bytes(xp.at[it, pl.ds(0, NK - FB)], xp_recv.at[it])
             point = jnp.int32(0)
             for i in range(1, 4):
                 point = jnp.where(any_of([PLUS_AT[c][4 * q + i] for c in range(2)]), i, point)
             onsets = onp_ref[pl.ds(4 * q + point, 1), :]
             send_chunk = scatter(it, ypsnd, wp.at[it, q, part * 4 + point], wp_send.at[it], wp_recv.at[it, q])
-            window(xp.at[it], onsets, ypsnd.at[it], send_chunk, far_first)
+            window(xp.at[it], onsets, ypsnd.at[it], send_chunk, far_first, xp_recv.at[it])
 
     def update(it, q):
         here = any_of(plus_places(q))

time: 114 us -> 113 us (level)
  Pallas kernels: 114 us -> 112 us
    pallas_call x1, Pallas kernels: 112 us -> 110 us  [local(): pl.pallas_call(kernel, out_shape=(jax.ShapeDtypeStruct((2 * FB, ML * PS),...]
where the time goes in v7:
time: 113 us
  Pallas kernels  112 us (99%)
    pallas_call x1, Pallas kernels, local(): pl.pallas_call(kernel, out_shape=(jax.ShapeDtypeStruct((2 * FB, ML * PS),...  110 us

profile of v7, /device:TPU:1, one launch (start us, length us, event | category | flops | bytes accessed | tf_op | source)
XLA Modules:
  0.0 113.0 jit_solution(753413732565534041)
XLA Ops:
  0.6 110.4 %shard_map.68 = (bf16[64,384]{1,0:T(8,128)(2,1)}, bf16[64,1536]{1,0:T(8,128)(2,1)}) custom-call(bf16[2048,1024]{1,0:T(8,128)(2,1)} %bitcast.6, f32[2,1024,1024]{2,1,0:T(8,128)} %constant.2.clone.tab_hbm, f32[64,1536]{1,0:T(8,128)} %bitcast.7, s32[12,32]{1,0:T(8,128)} %bitcast.9, s32[12,128]{1,0:T(8,128)} %bitcast.10), custom_call_target="tpu_custom_call" | custom-call | tf_op jit(solution)/shard_map/pallas_call | solution.py:525
  111.1 1.9 %shard_map.69 = (f32[64,384]{1,0:T(8,128)}, f32[64,1536]{1,0:T(8,128)}) custom-call(bf16[64,384]{1,0:T(8,128)(2,1)} %get-tuple-element.6.minus_ref, bf16[64,1536]{1,0:T(8,128)(2,1)} %get-tuple-element.7.change_ref, f32[64,1536]{1,0:T(8,128)} %bitcast.8), custom_call_target="tpu_custom_call" | custom-call | tf_op jit(solution)/shard_map/pallas_call | solution.py:580

commit v8 on v7

--- a/solution.py
+++ b/solution.py
@@ -325,6 +325,14 @@
         row_s = lax.broadcasted_iota(jnp.int32, (2 * FB, 1024), 0)
         lane_s = lax.broadcasted_iota(jnp.int32, (2 * FB, 1024), 1)
         wide[...] = jnp.where(lax.rem(row_s, GF) == lax.rem(lane_s // ML, GF), spread_rows, 0.0)
+        def send(x, y, start, rows, dst, sem, to):
+            src = partial.at[it, q, x, y, pl.ds(start, rows)]
+            remote_r(src, dst, rs_send.at[it], rs_recv.at[it, q, sem], to).start()
+
+        def send_half(k, i):
+            there = from_x.at[it, q, 1 - k, pl.ds(0, HALF)]
+            send(along_x(2), me_y, k * HALF, HALF, there, 2 - k, row_x(i))
+
         for g in range(NG):
             blocks = [wide[c * FB + g * GF : c * FB + (g + 1) * GF, :] for c in range(2)]
             re, im = [
@@ -339,18 +347,17 @@
                 out = out.astype(BF16)
                 for y in range(2):
                     partial[it, q, n, y, g * ROWS : (g + 1) * ROWS, :] = out[:, y * SL : (y + 1) * SL]
-
-        def send(x, y, start, rows, dst, sem, to):
-            src = partial.at[it, q, x, y, pl.ds(start, rows)]
-            remote_r(src, dst, rs_send.at[it], rs_recv.at[it, q, sem], to).start()
+            if g == 0:
+                for k, i in enumerate((1, 3)):
+                    there = from_x.at[it, q, 1 - k, pl.ds(HALF, ROWS)]
+                    send(along_x(i), 1 - me_y, 0, ROWS, there, 2 - k, row_x(i))
+            if g == 1:
+                send_half(0, 1)
 
         for k, i in enumerate((1, 3)):
             send(along_x(i), 1 - me_y, ROWS, 3 * ROWS, from_y.at[it, q, k], 3, beside)
         send(along_x(2), 1 - me_y, 0, 4 * ROWS, from_far.at[it, q], 0, row_x(2))
-        for k, i in enumerate((1, 3)):
-            there = from_x.at[it, q, 1 - k]
-            send(along_x(2), me_y, k * HALF, HALF, there.at[pl.ds(0, HALF)], 2 - k, row_x(i))
-            send(along_x(i), 1 - me_y, 0, ROWS, there.at[pl.ds(HALF, ROWS)], 2 - k, row_x(i))
+        send_half(1, 3)
 
     def pass_sums(it, q):
         def pass_on(total, slot, sem, to):

time: 113 us -> 113 us (level)
  no operation moved by 1% of the time
where the time goes in v8:
time: 113 us
  Pallas kernels  113 us (100%)
    pallas_call x1, Pallas kernels, local(): pl.pallas_call(kernel, out_shape=(jax.ShapeDtypeStruct((2 * FB, ML * PS),...  111 us

profile of v8, /device:TPU:1, one launch (start us, length us, event | category | flops | bytes accessed | tf_op | source)
XLA Modules:
  0.0 113.2 jit_solution(8082038725364829257)
XLA Ops:
  0.6 110.7 %shard_map.68 = (bf16[64,384]{1,0:T(8,128)(2,1)}, bf16[64,1536]{1,0:T(8,128)(2,1)}) custom-call(bf16[2048,1024]{1,0:T(8,128)(2,1)} %bitcast.6, f32[2,1024,1024]{2,1,0:T(8,128)} %constant.2.clone.tab_hbm, f32[64,1536]{1,0:T(8,128)} %bitcast.7, s32[12,32]{1,0:T(8,128)} %bitcast.9, s32[12,128]{1,0:T(8,128)} %bitcast.10), custom_call_target="tpu_custom_call" | custom-call | tf_op jit(solution)/shard_map/pallas_call | solution.py:532
  111.3 1.9 %shard_map.69 = (f32[64,384]{1,0:T(8,128)}, f32[64,1536]{1,0:T(8,128)}) custom-call(bf16[64,384]{1,0:T(8,128)(2,1)} %get-tuple-element.6.minus_ref, bf16[64,1536]{1,0:T(8,128)(2,1)} %get-tuple-element.7.change_ref, f32[64,1536]{1,0:T(8,128)} %bitcast.8), custom_call_target="tpu_custom_call" | custom-call | tf_op jit(solution)/shard_map/pallas_call | solution.py:587
